TPU v7x, 32 devices: a whole 2x2x4 slice. The times are simulated.
32 devices in a mesh: grp: 4 (over x, core), dev: 8 (over z, y).
Axes of the slice: x: 2, y: 2, z: 4, core: 2. Of those that a mesh axis runs over, the one named last changes fastest.
Arguments:
- fine_residual: bfloat16 [4, 8, 4, 4, 24, 2, 3072], P('grp', 'dev'), may hold values from -4 to 4
- near_null: bfloat16 [4, 8, 4, 4, 2, 32, 3072], P('grp', 'dev'), may hold values from -0.375 to 0.375
- coarse_operator: bfloat16 [4, 8, 4, 4, 64, 1152], P(None, 'dev'), may hold values from -1 to 7
Outputs:
- fine_correction: bfloat16 [4, 8, 4, 4, 24, 2, 3072], P('grp', 'dev')
- coarse_residual: float32 [4, 8, 4, 4, 24, 128], P('grp', 'dev')
All inputs are finite; a program needn't handle non-finite values.
Results may differ from a plain program's by a relative error of at most 0.012.
The roundings to bfloat16 on the way count: a program that leaves them out, or rounds other values in their place, can miss the bound.
Values may be sent and summed in bfloat16 or wider, within the bound.
No kernel may reach another device: no remote copies, remote signals or barrier semaphores. Data moves between devices by JAX's collectives and lax.ppermute only.
A program may use at most 128 MiB of HBM per device.

v0:
```python
import functools

import jax
import jax.numpy as jnp
from jax import lax
from jax.experimental import pallas as pl
from jax.experimental.pallas import tpu as pltpu
from jax.sharding import PartitionSpec as P

ITERS = 3
SHIFT = 3.0
LIMIT = 40 * 1024 * 1024
F32 = jnp.float32
BF16 = jnp.bfloat16
NT = (((1,), (1,)), ((), ()))
NN = (((1,), (0,)), ((), ()))
VM = pl.BlockSpec(memory_space=pltpu.VMEM)
ANY = pl.BlockSpec(memory_space=pl.ANY)
PARAMS = pltpu.CompilerParams(vmem_limit_bytes=LIMIT)


def pairings(count):
    if count % 2:
        ahead = [(i, (i - 1) % count) for i in range(count)]
        return ahead, [(target, source) for source, target in ahead]
    first = [(i, i ^ 1) for i in range(count)]
    second = [(i, (i + 1) % count if i % 2 else (i - 1) % count) for i in range(count)]
    return first, second


def swapped(axis):
    if lax.axis_size(axis) % 2:
        return jnp.bool_(False)
    return lax.rem(lax.axis_index(axis), 2) == 1


def exchange(high):
    planes = {}
    for axis in ("dev", "grp"):
        first, second = pairings(lax.axis_size(axis))
        planes[axis] = (lax.ppermute(high, axis, second), lax.ppermute(high, axis, first))
    return planes["grp"][1], planes["grp"][0], planes["dev"][1], planes["dev"][0]


def lanes(shape):
    return lax.broadcasted_iota(jnp.int32, shape, len(shape) - 1)


def stacked(vector):
    wide = vector.astype(F32)
    half = wide.shape[-1] // 2
    turned = pltpu.roll(wide, half, 1)
    sign = jnp.where(lanes(wide.shape) < half, 1.0, -1.0)
    return jnp.concatenate([wide * sign, turned], axis=0).astype(BF16)


def halves(value):
    high = value.astype(BF16)
    return high, (value - high.astype(F32)).astype(BF16)


def joined(product, rows):
    return jnp.concatenate([product[:rows], product[rows:]], axis=1)


def restrict_kernel(field_hbm, near_hbm, source_ref, high_ref, low_ref, near_ref, field, prods, sem):
    sites = field.shape[0]
    nrhs = field.shape[1]
    middle = field.shape[-1] // 2
    copies = []
    for s in range(sites):
        pair = (
            pltpu.make_async_copy(field_hbm.at[s], field.at[s], sem.at[0, s]),
            pltpu.make_async_copy(near_hbm.at[s], near_ref.at[s], sem.at[1, s]),
        )
        for copy in pair:
            copy.start()
        copies.append(pair)
    nvec = near_ref.shape[1] // 2
    for s in range(sites):
        for copy in copies[s]:
            copy.wait()
        fine = field[s].reshape(2 * nrhs, 2 * middle)
        near = near_ref[s]
        parts = [
            lax.dot_general(
                fine[:, h * middle : (h + 1) * middle],
                near[:, h * middle : (h + 1) * middle],
                NT,
                preferred_element_type=F32,
            )
            for h in range(2)
        ]
        prods[s] = jnp.concatenate(parts, axis=1)
    for s in range(sites):
        even = prods[s, pl.ds(0, nrhs, 2), :]
        odd = prods[s, pl.ds(1, nrhs, 2), :]
        wide = 4 * nvec
        real = even + pltpu.roll(odd, wide - nvec, 1)
        imag = odd - pltpu.roll(even, wide - nvec, 1)
        lane = lanes(real.shape)
        value = jnp.where(
            lane < nvec,
            real,
            jnp.where(
                lane < 2 * nvec,
                pltpu.roll(real, wide - nvec, 1),
                jnp.where(lane < 3 * nvec, pltpu.roll(imag, 2 * nvec, 1), pltpu.roll(imag, nvec, 1)),
            ),
        )
        source_ref[s] = value
        high, low = halves(value)
        high_ref[s] = high
        low_ref[s] = low


def restrict(field, near):
    sites, nrhs, _, fine = field.shape
    coarse = 2 * near.shape[1]
    return pl.pallas_call(
        restrict_kernel,
        in_specs=[ANY, ANY],
        out_specs=[VM] * 4,
        out_shape=[
            jax.ShapeDtypeStruct((sites, nrhs, coarse), F32),
            jax.ShapeDtypeStruct((sites, nrhs, coarse), BF16),
            jax.ShapeDtypeStruct((sites, nrhs, coarse), BF16),
            jax.ShapeDtypeStruct(near.shape, BF16),
        ],
        scratch_shapes=[
            pltpu.VMEM(field.shape, BF16),
            pltpu.VMEM((sites, 2 * nrhs, coarse), F32),
            pltpu.SemaphoreType.DMA((2, sites)),
        ],
        compiler_params=PARAMS,
        name="restrict",
    )(field, near)


def neighbours(s, ly, lx):
    y, x = s // lx, s % lx
    return [((y + 1) % ly) * lx + x, ((y - 1) % ly) * lx + x, y * lx + (x + 1) % lx, y * lx + (x - 1) % lx]


def local_product(s, dims, blocks, xy, extra):
    rows = xy.shape[1]
    wide = xy.shape[2]
    centre = lax.dot_general(
        jnp.concatenate([xy[s]] + [stacked(e) for e in extra], axis=0),
        blocks[:, :wide],
        NT,
        preferred_element_type=F32,
    )
    sides = lax.dot_general(
        jnp.concatenate([xy[j] for j in neighbours(s, *dims)], axis=1),
        blocks[:, 5 * wide :],
        NT,
        preferred_element_type=F32,
    )
    total = centre[:rows] + sides
    return total, [centre[(i + 1) * rows : (i + 2) * rows] for i in range(len(extra))]


def first_local_kernel(dims, high, low, oper_hbm, part_ref, rest_ref, oper_ref, xy, sem):
    sites = xy.shape[0]
    copies = []
    plane = lax.axis_index("grp")
    for s in range(sites):
        copy = pltpu.make_async_copy(oper_hbm.at[plane, s], oper_ref.at[s], sem.at[s])
        copy.start()
        copies.append(copy)
    for s in range(sites):
        xy[s] = stacked(high[s])
    rows = high.shape[1]
    for s in range(sites):
        copies[s].wait()
        total, extra = local_product(s, dims, oper_ref[s], xy, [low[s]])
        part_ref[s] = joined(total, rows)
        rest_ref[s] = joined(extra[0], rows)


def later_local_kernel(dims, with_rest, high, low, *refs):
    if with_rest:
        rest, oper_ref, part_ref, rest_out, xy = refs
    else:
        oper_ref, part_ref, xy = refs
    sites = xy.shape[0]
    rows = high.shape[1]
    for s in range(sites):
        xy[s] = stacked(high[s])
    for s in range(sites):
        extra = [low[s]] + ([rest[s]] if with_rest else [])
        total, more = local_product(s, dims, oper_ref[s], xy, extra)
        part_ref[s] = joined(total + more[0], rows)
        if with_rest:
            rest_out[s] = joined(more[1], rows)


def halo_value(s, flips, planes, part, before, oper_ref):
    rows, wide = part.shape[1], part.shape[2]
    cols = []
    for flip, (one, two) in zip(flips, planes):
        a, b = one[s].astype(F32), two[s].astype(F32)
        cols.append(stacked(jnp.where(flip, b, a)))
        cols.append(stacked(jnp.where(flip, a, b)))
    product = lax.dot_general(
        jnp.concatenate(cols, axis=1), oper_ref[s, :, wide : 5 * wide], NT, preferred_element_type=F32
    )
    return part[s] + joined(product, rows) - SHIFT * before[s]


def halo_kernel(t_one, t_two, z_one, z_two, part, before, oper_ref, value_ref, high_ref, low_ref):
    flips = (swapped("grp"), swapped("dev"))
    for s in range(part.shape[0]):
        value = halo_value(s, flips, ((t_one, t_two), (z_one, z_two)), part, before, oper_ref)
        value_ref[s] = value
        high_ref[s], low_ref[s] = halves(value)


def slots(count):
    table = {}
    for i in range(count):
        for j in range(i, count):
            table[(i, j, 0)] = len(table)
            if j > i:
                table[(i, j, 1)] = len(table)
    return table


def last_kernel(t_one, t_two, z_one, z_two, part, r0, v1, w1, v2, w2, oper_ref, v3, sums_ref):
    flips = (swapped("grp"), swapped("dev"))
    sites, rows, wide = part.shape
    half = wide // 2
    for s in range(sites):
        v3[s] = halo_value(s, flips, ((t_one, t_two), (z_one, z_two)), part, v2, oper_ref)
    basis = [r0, v1, w1, v2, w2, v3]
    table = slots(len(basis))
    total = {key: jnp.zeros((rows, wide), F32) for key in table}
    for s in range(sites):
        plain = [b[s] for b in basis]
        turned = [pltpu.roll(p, half, 1) for p in plain]
        for i, j, part_of in table:
            total[(i, j, part_of)] += plain[i] * (turned[j] if part_of else plain[j])
    sign = jnp.where(lanes((rows, wide)) < half, 1.0, -1.0)
    lane = lanes((rows, wide))
    packed = jnp.zeros((rows, wide), F32)
    for key, slot in table.items():
        value = total[key] * sign if key[2] else total[key]
        packed = jnp.where(lane == slot, jnp.sum(value, axis=1, keepdims=True), packed)
    square = jnp.concatenate([packed, jnp.zeros((wide - rows, wide), F32)], axis=0).T
    dense = jnp.zeros((8, wide), F32)
    for group in range(-(-len(table) // 8)):
        piece = square[8 * group : 8 * group + 8]
        dense = dense + (pltpu.roll(piece, rows * group, 1) if group else piece)
    for d in range(sums_ref.shape[0]):
        sums_ref[d] = dense


def times(a, b):
    return (a[0] * b[0] - a[1] * b[1], a[0] * b[1] + a[1] * b[0])


def plus(a, b):
    return (a[0] + b[0], a[1] + b[1])


def minus(a, b):
    return (a[0] - b[0], a[1] - b[1])


def over(a, b):
    return (a[0] / b, a[1] / b)


def combine(a, b, op):
    out = []
    for x, y in zip(a, b):
        if y is None:
            out.append(x)
        elif x is None:
            out.append(y if op is plus else (-y[0], -y[1]))
        else:
            out.append(op(x, y))
    return out


def scale(c, a):
    return [None if x is None else times(c, x) for x in a]


def recurrences(gram, one):
    zero = jnp.zeros_like(one)

    def entry(i, j):
        if i == j:
            return (gram[(i, i, 0)], zero)
        if i < j:
            return (gram[(i, j, 0)], gram[(i, j, 1)])
        return (gram[(j, i, 0)], -gram[(j, i, 1)])

    count = 6

    def lower(a):
        out = []
        for i in range(count):
            total = (zero, zero)
            for j in range(count):
                if a[j] is not None:
                    total = plus(total, times(entry(i, j), a[j]))
            out.append(total)
        return out

    def inner(a, lowered):
        total = (zero, zero)
        for x, y in zip(a, lowered):
            if x is not None:
                total = plus(total, times((x[0], -x[1]), y))
        return total

    def apply(a, rounded):
        out = [None] * count
        shift = lambda x: (SHIFT * x[0], SHIFT * x[1])
        for source, target in ((0, 1), (1, 3), (3, 5)):
            if a[source] is not None:
                out = combine(out, [shift(a[source]) if k == source else None for k in range(count)], plus)
                out = combine(out, [a[source] if k == target else None for k in range(count)], plus)
        if a[0] is not None and not rounded:
            out = combine(out, [a[0] if k == 2 else None for k in range(count)], plus)
        if a[2] is not None:
            out = combine(out, [a[2] if k == 4 else None for k in range(count)], plus)
        return out

    residual = [(one, zero)] + [None] * (count - 1)
    answer = [None] * count
    directions, images, lows, curvatures = [], [], [], []
    for iteration in range(ITERS):
        direction = residual
        image = apply(direction, iteration == 0)
        factors = [over(inner(image, low), c) for low, c in zip(lows, curvatures)]
        factors = [(f[0], -f[1]) for f in factors]
        for f, p, q in zip(factors, directions, images):
            image = combine(image, scale(f, q), minus)
            direction = combine(direction, scale(f, p), minus)
        low = lower(image)
        curvature = inner(image, low)[0]
        along = inner(residual, low)
        step = over((along[0], -along[1]), curvature)
        answer = combine(answer, scale(step, direction), plus)
        residual = combine(residual, scale(step, image), minus)
        directions.append(direction)
        images.append(image)
        lows.append(low)
        curvatures.append(curvature)
    return answer, residual


def finish_kernel(sums, r0, v1, w1, v2, w2, v3, near, fine_hbm, resid_ref, coef, fine, sem):
    sites, rows, wide = r0.shape
    half = wide // 2
    quarter = half // 2
    middle = near.shape[-1] // 2
    dense = sums[0]
    for d in range(1, sums.shape[0]):
        dense = dense + sums[d]
    basis = [r0, v1, w1, v2, w2, v3]
    table = slots(len(basis))
    turned = [dense if g == 0 else pltpu.roll(dense, wide - rows * g, 1) for g in range(-(-len(table) // 8))]
    gram = {key: turned[slot // 8][slot % 8 : slot % 8 + 1] for key, slot in table.items()}
    answer, residual = recurrences(gram, jnp.ones((1, wide), F32))
    entries = []
    for which, coords in ((0, answer), (1, residual)):
        for index, value in enumerate(coords):
            if value is not None:
                entries.append((which, index, value))
    coef[...] = jnp.zeros_like(coef)
    for e, (_, _, value) in enumerate(entries):
        coef[2 * e : 2 * e + 1] = value[0]
        coef[2 * e + 1 : 2 * e + 2] = value[1]
    columns = coef[...].T[:rows]
    sign = jnp.where(lanes((rows, wide)) < half, -1.0, 1.0)
    spread = [
        (
            which,
            index,
            jnp.broadcast_to(columns[:, 2 * e : 2 * e + 1], (rows, wide)),
            jnp.broadcast_to(columns[:, 2 * e + 1 : 2 * e + 2], (rows, wide)) * sign,
        )
        for e, (which, index, _) in enumerate(entries)
    ]
    lane = lanes((rows, wide))
    copies = []
    for s in range(sites):
        plain = [b[s] for b in basis]
        rolled = [pltpu.roll(p, half, 1) for p in plain]
        out = [jnp.zeros((rows, wide), F32), jnp.zeros((rows, wide), F32)]
        for which, index, re, im in spread:
            out[which] = out[which] + re * plain[index] + im * rolled[index]
        resid_ref[s] = out[1]
        x = out[0].astype(BF16).astype(F32)
        by1 = pltpu.roll(x, wide - quarter, 1)
        by2 = pltpu.roll(x, half, 1)
        by3 = pltpu.roll(x, quarter, 1)
        upper = (jnp.where(lane < quarter, x, -by1), jnp.where(lane < quarter, by2, by3))
        lower = (jnp.where(lane < quarter, by1, -by2), jnp.where(lane < quarter, by3, x))
        for h, (first, second) in enumerate((upper, lower)):
            mixed = jnp.stack([first, second], axis=1).reshape(2 * rows, wide)[:, :half].astype(BF16)
            product = lax.dot_general(
                mixed, near[s, :, h * middle : (h + 1) * middle], NN, preferred_element_type=F32
            )
            fine[s, :, :, h * middle : (h + 1) * middle] = product.astype(BF16).reshape(rows, 2, middle)
        copy = pltpu.make_async_copy(fine.at[s], fine_hbm.at[s], sem.at[s])
        copy.start()
        copies.append(copy)
    for copy in copies:
        copy.wait()


def on_device(fine_residual, near_null, coarse_operator):
    ly, lx, nrhs, _, fine = fine_residual.shape[2:]
    sites = ly * lx
    nvec = near_null.shape[-2]
    wide = 4 * nvec
    field = fine_residual.reshape(sites, nrhs, 2, fine)
    near = near_null.reshape(sites, 2 * nvec, fine)
    oper = coarse_operator.reshape((-1, sites) + coarse_operator.shape[-2:])
    dims = (ly, lx)
    vector = jax.ShapeDtypeStruct((sites, nrhs, wide), F32)
    rounded = jax.ShapeDtypeStruct((sites, nrhs, wide), BF16)
    xy = pltpu.VMEM((sites, 2 * nrhs, wide), BF16)

    r0, h0, l0, near = restrict(field, near)

    planes = exchange(h0)
    part, w1, oper = pl.pallas_call(
        functools.partial(first_local_kernel, dims),
        in_specs=[VM, VM, ANY],
        out_specs=[VM] * 3,
        out_shape=[vector, vector, jax.ShapeDtypeStruct(oper.shape[1:], BF16)],
        scratch_shapes=[xy, pltpu.SemaphoreType.DMA((sites,))],
        compiler_params=PARAMS,
        name="local_1",
    )(h0, l0, oper)
    v1, h1, l1 = pl.pallas_call(
        halo_kernel,
        in_specs=[VM] * 7,
        out_specs=[VM] * 3,
        out_shape=[vector, rounded, rounded],
        compiler_params=PARAMS,
        name="halo_1",
    )(*planes, part, r0, oper)

    planes = exchange(h1)
    part, w2 = pl.pallas_call(
        functools.partial(later_local_kernel, dims, True),
        in_specs=[VM] * 4,
        out_specs=[VM] * 2,
        out_shape=[vector, vector],
        scratch_shapes=[xy],
        compiler_params=PARAMS,
        name="local_2",
    )(h1, l1, w1, oper)
    v2, h2, l2 = pl.pallas_call(
        halo_kernel,
        in_specs=[VM] * 7,
        out_specs=[VM] * 3,
        out_shape=[vector, rounded, rounded],
        compiler_params=PARAMS,
        name="halo_2",
    )(*planes, part, v1, oper)

    planes = exchange(h2)
    part = pl.pallas_call(
        functools.partial(later_local_kernel, dims, False),
        in_specs=[VM] * 3,
        out_specs=VM,
        out_shape=vector,
        scratch_shapes=[xy],
        compiler_params=PARAMS,
        name="local_3",
    )(h2, l2, oper)
    devices = lax.axis_size("grp") * lax.axis_size("dev")
    v3, sums = pl.pallas_call(
        last_kernel,
        in_specs=[VM] * 11,
        out_specs=[VM] * 2,
        out_shape=[vector, jax.ShapeDtypeStruct((devices, 8, wide), F32)],
        compiler_params=PARAMS,
        name="halo_3",
    )(*planes, part, r0, v1, w1, v2, w2, oper)

    sums = lax.all_to_all(sums, ("grp", "dev"), 0, 0)
    correction, residual = pl.pallas_call(
        finish_kernel,
        in_specs=[VM] * 8,
        out_specs=[ANY, VM],
        out_shape=[jax.ShapeDtypeStruct(field.shape, BF16), vector],
        scratch_shapes=[
            pltpu.VMEM((wide, wide), F32),
            pltpu.VMEM(field.shape, BF16),
            pltpu.SemaphoreType.DMA((sites,)),
        ],
        compiler_params=PARAMS,
        name="finish",
    )(sums, r0, v1, w1, v2, w2, v3, near)
    return correction.reshape(fine_residual.shape), residual.reshape((1, 1, ly, lx, nrhs, wide))


def solution(mesh):
    in_specs = (
        P("grp", "dev", None, None, None, None, None),
        P("grp", "dev", None, None, None, None, None),
        P(None, "dev", None, None, None, None),
    )
    out_specs = (
        P("grp", "dev", None, None, None, None, None),
        P("grp", "dev", None, None, None, None),
    )
    return jax.shard_map(
        on_device, mesh=mesh, in_specs=in_specs, out_specs=out_specs, check_vma=False
    )
```

profile of v0, /device:TPU:0, one launch (start us, length us, event | category | flops | bytes accessed | tf_op | source)
XLA Modules:
  0.0 63.1 jit_solution(12904671545768707645)
XLA Ops:
  0.6 2.5 %copy-done.2 = bf16[1,1,4,4,24,2,3072]{6,5,4,3,2,1,0:T(2,128)(2,1)S(1)} copy-done((bf16[1,1,4,4,24,2,3072]{6,5,4,3,2,1,0:T(2,128)(2,1)S(1)}, bf16[1,1,4,4,24,2,3072]{6,5,4,3,2,1,0:T(2,128)(2,1)}, u32[]{:S(2)}) %copy-start.2) | copy-done | bytes 4718616
  3.1 7.2 %restrict.1 = (f32[16,24,128]{2,1,0:T(8,128)S(1)}, bf16[16,24,128]{2,1,0:T(8,128)(2,1)S(1)}, bf16[16,24,128]{2,1,0:T(8,128)(2,1)S(1)}, bf16[16,64,3072]{2,1,0:T(8,128)(2,1)S(1)}) custom-call(bf16[16,24,2,3072]{3,2,1,0:T(2,128)(2,1)S(1)} %bitcast.8, bf16[16,64,3072]{2,1,0:T(8,128)(2,1)} %bitcast.9), custom_call_target="tpu_custom_call" | custom-call | tf_op jit(solution)/shard_map/restrict/pallas_call | solution.py:120
  10.4 2.6 %copy-done.1 = bf16[16,64,3072]{2,1,0:T(8,128)(2,1)} copy-done((bf16[16,64,3072]{2,1,0:T(8,128)(2,1)}, bf16[16,64,3072]{2,1,0:T(8,128)(2,1)S(1)}, u32[]{:S(2)}) %copy-start.1) | copy-done | bytes 6291480
  13.0 6.0 %collective-permute-start.3 = (bf16[16,24,128]{2,1,0:T(8,128)(2,1)S(1)}, bf16[16,24,128]{2,1,0:T(8,128)(2,1)S(1)}, u32[]{:S(2)}, u32[]{:S(2)}) collective-permute-start(bf16[16,24,128]{2,1,0:T(8,128)(2,1)S(1)} %get-tuple-element.21.high), channel_id=1, source_target_pairs={{0,7},{1,2},{2,1},{3,4},{4,3},{5,6},{6,5},{7,0},{8,15},{9,10},{10,... | collective-permute-start | bytes 294920 | tf_op jit(solution)/shard_map/ppermute | solution.py:41
  19.0 0.7 %collective-permute-start.1 = (bf16[16,24,128]{2,1,0:T(8,128)(2,1)S(1)}, bf16[16,24,128]{2,1,0:T(8,128)(2,1)S(1)}, u32[]{:S(2)}, u32[]{:S(2)}) collective-permute-start(bf16[16,24,128]{2,1,0:T(8,128)(2,1)S(1)} %get-tuple-element.21.high), channel_id=1, source_target_pairs={{0,24},{8,16},{16,8},{24,0},{1,25},{9,17},{17,9},{25,1},{2,26},{10... | collective-permute-start | bytes 294920 | tf_op jit(solution)/shard_map/ppermute | solution.py:41
  19.7 1.0 %collective-permute-start = (bf16[16,24,128]{2,1,0:T(8,128)(2,1)S(1)}, bf16[16,24,128]{2,1,0:T(8,128)(2,1)S(1)}, u32[]{:S(2)}, u32[]{:S(2)}) collective-permute-start(bf16[16,24,128]{2,1,0:T(8,128)(2,1)S(1)} %get-tuple-element.21.high), channel_id=1, source_target_pairs={{0,8},{8,0},{16,24},{24,16},{1,9},{9,1},{17,25},{25,17},{2,10},{10... | collective-permute-start | bytes 294920 | tf_op jit(solution)/shard_map/ppermute | solution.py:41
  20.6 7.9 %local_1.1 = (f32[16,24,128]{2,1,0:T(8,128)S(1)}, f32[16,24,128]{2,1,0:T(8,128)S(1)}, bf16[16,64,1152]{2,1,0:T(8,128)(2,1)S(1)}) custom-call(bf16[16,24,128]{2,1,0:T(8,128)(2,1)S(1)} %get-tuple-element.21.high, bf16[16,24,128]{2,1,0:T(8,128)(2,1)S(1)} %get-tuple-element.22.low, bf16[4,16,64,1152]{3,2,1,0:T(8,128)(2,1)S(1)} %bitcast.5), custom_call_target="tpu_custom_call" | custom-call | tf_op jit(solution)/shard_map/local_1/pallas_call | solution.py:434
  28.6 0.0 collective-permute-done.3.z_two
  28.6 0.6 halo_1.1
  29.2 2.0 %collective-permute-start.7 = (bf16[16,24,128]{2,1,0:T(8,128)(2,1)S(1)}, bf16[16,24,128]{2,1,0:T(8,128)(2,1)S(1)}, u32[]{:S(2)}, u32[]{:S(2)}) collective-permute-start(bf16[16,24,128]{2,1,0:T(8,128)(2,1)S(1)} %get-tuple-element.26.high), channel_id=1, source_target_pairs={{0,7},{1,2},{2,1},{3,4},{4,3},{5,6},{6,5},{7,0},{8,15},{9,10},{10,... | collective-permute-start | bytes 294920 | tf_op jit(solution)/shard_map/ppermute | solution.py:41
  31.2 0.2 collective-permute-start.6
  31.4 0.6 %collective-permute-start.4 = (bf16[16,24,128]{2,1,0:T(8,128)(2,1)S(1)}, bf16[16,24,128]{2,1,0:T(8,128)(2,1)S(1)}, u32[]{:S(2)}, u32[]{:S(2)}) collective-permute-start(bf16[16,24,128]{2,1,0:T(8,128)(2,1)S(1)} %get-tuple-element.26.high), channel_id=1, source_target_pairs={{0,8},{8,0},{16,24},{24,16},{1,9},{9,1},{17,25},{25,17},{2,10},{10... | collective-permute-start | bytes 294920 | tf_op jit(solution)/shard_map/ppermute | solution.py:41
  32.0 0.9 %local_2.1 = (f32[16,24,128]{2,1,0:T(8,128)S(1)}, f32[16,24,128]{2,1,0:T(8,128)S(1)}) custom-call(bf16[16,24,128]{2,1,0:T(8,128)(2,1)S(1)} %get-tuple-element.26.high, bf16[16,24,128]{2,1,0:T(8,128)(2,1)S(1)} %get-tuple-element.27.low, f32[16,24,128]{2,1,0:T(8,128)S(1)} %get-tuple-element.28.refs_0_.w1, ...), custom_call_target="tpu_custom_call" | custom-call | tf_op jit(solution)/shard_map/local_2/pallas_call | solution.py:453
  32.9 3.9 %collective-permute-done.7.z_two = bf16[16,24,128]{2,1,0:T(8,128)(2,1)S(1)} collective-permute-done((bf16[16,24,128]{2,1,0:T(8,128)(2,1)S(1)}, bf16[16,24,128]{2,1,0:T(8,128)(2,1)S(1)}, u32[]{:S(2)}, u32[]{:S(2)}) %collective-permute-start.7) | collective-permute-done | bytes 98336 | tf_op jit(solution)/shard_map/ppermute | solution.py:41
  36.8 0.9 %collective-permute-done.6.z_one = bf16[16,24,128]{2,1,0:T(8,128)(2,1)S(1)} collective-permute-done((bf16[16,24,128]{2,1,0:T(8,128)(2,1)S(1)}, bf16[16,24,128]{2,1,0:T(8,128)(2,1)S(1)}, u32[]{:S(2)}, u32[]{:S(2)}) %collective-permute-start.6) | collective-permute-done | bytes 98336 | tf_op jit(solution)/shard_map/ppermute | solution.py:41
  37.7 0.6 halo_2.1
  38.3 2.9 %collective-permute-start.11 = (bf16[16,24,128]{2,1,0:T(8,128)(2,1)S(1)}, bf16[16,24,128]{2,1,0:T(8,128)(2,1)S(1)}, u32[]{:S(2)}, u32[]{:S(2)}) collective-permute-start(bf16[16,24,128]{2,1,0:T(8,128)(2,1)S(1)} %get-tuple-element.31.high), channel_id=1, source_target_pairs={{0,7},{1,2},{2,1},{3,4},{4,3},{5,6},{6,5},{7,0},{8,15},{9,10},{10,... | collective-permute-start | bytes 294920 | tf_op jit(solution)/shard_map/ppermute | solution.py:41
  41.2 0.6 %collective-permute-start.8 = (bf16[16,24,128]{2,1,0:T(8,128)(2,1)S(1)}, bf16[16,24,128]{2,1,0:T(8,128)(2,1)S(1)}, u32[]{:S(2)}, u32[]{:S(2)}) collective-permute-start(bf16[16,24,128]{2,1,0:T(8,128)(2,1)S(1)} %get-tuple-element.31.high), channel_id=1, source_target_pairs={{0,8},{8,0},{16,24},{24,16},{1,9},{9,1},{17,25},{25,17},{2,10},{10... | collective-permute-start | bytes 294920 | tf_op jit(solution)/shard_map/ppermute | solution.py:41
  41.8 0.7 %local_3.1.part = f32[16,24,128]{2,1,0:T(8,128)S(1)} custom-call(bf16[16,24,128]{2,1,0:T(8,128)(2,1)S(1)} %get-tuple-element.31.high, bf16[16,24,128]{2,1,0:T(8,128)(2,1)S(1)} %get-tuple-element.32.low, bf16[16,64,1152]{2,1,0:T(8,128)(2,1)S(1)} %get-tuple-element.25.oper_ref.refs_1_.refs_0_), custom_call_target="tpu_custom_call" | custom-call | tf_op jit(solution)/shard_map/local_3/pallas_call | solution.py:472
  42.5 3.3 %collective-permute-done.11.z_two = bf16[16,24,128]{2,1,0:T(8,128)(2,1)S(1)} collective-permute-done((bf16[16,24,128]{2,1,0:T(8,128)(2,1)S(1)}, bf16[16,24,128]{2,1,0:T(8,128)(2,1)S(1)}, u32[]{:S(2)}, u32[]{:S(2)}) %collective-permute-start.11) | collective-permute-done | bytes 98336 | tf_op jit(solution)/shard_map/ppermute | solution.py:41
  45.8 0.9 %collective-permute-done.10.z_one = bf16[16,24,128]{2,1,0:T(8,128)(2,1)S(1)} collective-permute-done((bf16[16,24,128]{2,1,0:T(8,128)(2,1)S(1)}, bf16[16,24,128]{2,1,0:T(8,128)(2,1)S(1)}, u32[]{:S(2)}, u32[]{:S(2)}) %collective-permute-start.10) | collective-permute-done | bytes 98336 | tf_op jit(solution)/shard_map/ppermute | solution.py:41
  46.7 1.1 %halo_3.1 = (f32[16,24,128]{2,1,0:T(8,128)S(1)}, f32[32,8,128]{2,1,0:T(8,128)S(1)}) custom-call(bf16[16,24,128]{2,1,0:T(8,128)(2,1)S(1)} %collective-permute-done.8.t_one, bf16[16,24,128]{2,1,0:T(8,128)(2,1)S(1)} %collective-permute-done.9.t_two, bf16[16,24,128]{2,1,0:T(8,128)(2,1)S(1)} %collective-permute-done.10.z_one, ...), custom_call_target="tpu_custom_call" | custom-call | tf_op jit(solution)/shard_map/halo_3/pallas_call | solution.py:482
  47.8 10.6 %all_to_all.5.sums = f32[32,8,128]{2,1,0:T(8,128)S(1)} all-to-all(f32[32,8,128]{2,1,0:T(8,128)S(1)} %get-tuple-element.35), channel_id=1, replica_groups=mesh['grp'=4,'dev'=8] {'grp','dev'}, dimensions={0} | all-to-all | bytes 262144 | tf_op jit(solution)/shard_map/all_to_all | solution.py:491
  58.5 4.6 %finish.1 = (bf16[16,24,2,3072]{3,2,1,0:T(2,128)(2,1)}, f32[16,24,128]{2,1,0:T(8,128)}) custom-call(f32[32,8,128]{2,1,0:T(8,128)S(1)} %all_to_all.5.sums, f32[16,24,128]{2,1,0:T(8,128)S(1)} %get-tuple-element.24.before.r0, f32[16,24,128]{2,1,0:T(8,128)S(1)} %get-tuple-element.30.before.v1, f32[16,24,128]{2,1,0:T(8,128)S(1)} %get-tuple-element.28.refs_0_.w1, ...), custom_call_target="tpu_custom_call" | custom-call | tf_op jit(solution)/shard_map/finish/pallas_call | solution.py:492
  (20 shorter events, 0.0 us)
Async XLA Ops:
  0.6 20.0 %copy-start = (bf16[4,1,4,4,64,1152]{5,4,3,2,1,0:T(8,128)(2,1)S(1)}, bf16[4,1,4,4,64,1152]{5,4,3,2,1,0:T(8,128)(2,1)}, u32[]{:S(2)}) copy-start(bf16[4,1,4,4,64,1152]{5,4,3,2,1,0:T(8,128)(2,1)} %param.5) | copy-start | bytes 28311556
  0.6 2.5 %copy-start.2 = (bf16[1,1,4,4,24,2,3072]{6,5,4,3,2,1,0:T(2,128)(2,1)S(1)}, bf16[1,1,4,4,24,2,3072]{6,5,4,3,2,1,0:T(2,128)(2,1)}, u32[]{:S(2)}) copy-start(bf16[1,1,4,4,24,2,3072]{6,5,4,3,2,1,0:T(2,128)(2,1)} %param.3) | copy-start | bytes 14155780
  10.3 2.7 %copy-start.1 = (bf16[16,64,3072]{2,1,0:T(8,128)(2,1)}, bf16[16,64,3072]{2,1,0:T(8,128)(2,1)S(1)}, u32[]{:S(2)}) copy-start(bf16[16,64,3072]{2,1,0:T(8,128)(2,1)S(1)} %get-tuple-element.37.near) | copy-start | bytes 18874372
  13.0 15.6 %collective-permute-start.3 = (bf16[16,24,128]{2,1,0:T(8,128)(2,1)S(1)}, bf16[16,24,128]{2,1,0:T(8,128)(2,1)S(1)}, u32[]{:S(2)}, u32[]{:S(2)}) collective-permute-start(bf16[16,24,128]{2,1,0:T(8,128)(2,1)S(1)} %get-tuple-element.21.high), channel_id=1, source_target_pairs={{0,7},{1,2},{2,1},{3,4},{4,3},{5,6},{6,5},{7,0},{8,15},{9,10},{10,... | collective-permute-start | bytes 294920 | tf_op jit(solution)/shard_map/ppermute | solution.py:41
  19.0 9.6 %collective-permute-start.2 = (bf16[16,24,128]{2,1,0:T(8,128)(2,1)S(1)}, bf16[16,24,128]{2,1,0:T(8,128)(2,1)S(1)}, u32[]{:S(2)}, u32[]{:S(2)}) collective-permute-start(bf16[16,24,128]{2,1,0:T(8,128)(2,1)S(1)} %get-tuple-element.21.high), channel_id=1, source_target_pairs={{0,1},{1,0},{2,3},{3,2},{4,5},{5,4},{6,7},{7,6},{8,9},{9,8},{10,11... | collective-permute-start | bytes 294920 | tf_op jit(solution)/shard_map/ppermute | solution.py:41
  19.0 9.6 %collective-permute-start.1 = (bf16[16,24,128]{2,1,0:T(8,128)(2,1)S(1)}, bf16[16,24,128]{2,1,0:T(8,128)(2,1)S(1)}, u32[]{:S(2)}, u32[]{:S(2)}) collective-permute-start(bf16[16,24,128]{2,1,0:T(8,128)(2,1)S(1)} %get-tuple-element.21.high), channel_id=1, source_target_pairs={{0,24},{8,16},{16,8},{24,0},{1,25},{9,17},{17,9},{25,1},{2,26},{10... | collective-permute-start | bytes 294920 | tf_op jit(solution)/shard_map/ppermute | solution.py:41
  19.7 8.9 %collective-permute-start = (bf16[16,24,128]{2,1,0:T(8,128)(2,1)S(1)}, bf16[16,24,128]{2,1,0:T(8,128)(2,1)S(1)}, u32[]{:S(2)}, u32[]{:S(2)}) collective-permute-start(bf16[16,24,128]{2,1,0:T(8,128)(2,1)S(1)} %get-tuple-element.21.high), channel_id=1, source_target_pairs={{0,8},{8,0},{16,24},{24,16},{1,9},{9,1},{17,25},{25,17},{2,10},{10... | collective-permute-start | bytes 294920 | tf_op jit(solution)/shard_map/ppermute | solution.py:41
  28.6 29.9 %slice-start = ((s8[6291456]{0:T(1024)(128)(4,1)}), s8[4194304]{0:T(1024)(128)(4,1)S(1)}, s32[]{:S(2)}) async-start(s8[6291456]{0:T(1024)(128)(4,1)} %bitcast.6), calls=%async_computation.1 | async-start | bytes 8388608
  29.2 7.6 %collective-permute-start.7 = (bf16[16,24,128]{2,1,0:T(8,128)(2,1)S(1)}, bf16[16,24,128]{2,1,0:T(8,128)(2,1)S(1)}, u32[]{:S(2)}, u32[]{:S(2)}) collective-permute-start(bf16[16,24,128]{2,1,0:T(8,128)(2,1)S(1)} %get-tuple-element.26.high), channel_id=1, source_target_pairs={{0,7},{1,2},{2,1},{3,4},{4,3},{5,6},{6,5},{7,0},{8,15},{9,10},{10,... | collective-permute-start | bytes 294920 | tf_op jit(solution)/shard_map/ppermute | solution.py:41
  31.2 6.6 %collective-permute-start.6 = (bf16[16,24,128]{2,1,0:T(8,128)(2,1)S(1)}, bf16[16,24,128]{2,1,0:T(8,128)(2,1)S(1)}, u32[]{:S(2)}, u32[]{:S(2)}) collective-permute-start(bf16[16,24,128]{2,1,0:T(8,128)(2,1)S(1)} %get-tuple-element.26.high), channel_id=1, source_target_pairs={{0,1},{1,0},{2,3},{3,2},{4,5},{5,4},{6,7},{7,6},{8,9},{9,8},{10,11... | collective-permute-start | bytes 294920 | tf_op jit(solution)/shard_map/ppermute | solution.py:41
  31.4 6.4 %collective-permute-start.5 = (bf16[16,24,128]{2,1,0:T(8,128)(2,1)S(1)}, bf16[16,24,128]{2,1,0:T(8,128)(2,1)S(1)}, u32[]{:S(2)}, u32[]{:S(2)}) collective-permute-start(bf16[16,24,128]{2,1,0:T(8,128)(2,1)S(1)} %get-tuple-element.26.high), channel_id=1, source_target_pairs={{0,24},{8,16},{16,8},{24,0},{1,25},{9,17},{17,9},{25,1},{2,26},{10... | collective-permute-start | bytes 294920 | tf_op jit(solution)/shard_map/ppermute | solution.py:41
  31.4 6.4 %collective-permute-start.4 = (bf16[16,24,128]{2,1,0:T(8,128)(2,1)S(1)}, bf16[16,24,128]{2,1,0:T(8,128)(2,1)S(1)}, u32[]{:S(2)}, u32[]{:S(2)}) collective-permute-start(bf16[16,24,128]{2,1,0:T(8,128)(2,1)S(1)} %get-tuple-element.26.high), channel_id=1, source_target_pairs={{0,8},{8,0},{16,24},{24,16},{1,9},{9,1},{17,25},{25,17},{2,10},{10... | collective-permute-start | bytes 294920 | tf_op jit(solution)/shard_map/ppermute | solution.py:41
  37.7 20.7 %slice-start.1 = ((s8[6291456]{0:T(1024)(128)(4,1)}), s8[2097152]{0:T(1024)(128)(4,1)S(1)}, s32[]{:S(2)}) async-start(s8[6291456]{0:T(1024)(128)(4,1)} %bitcast.6), calls=%async_computation.2 | async-start | bytes 4194304
  38.3 7.5 %collective-permute-start.11 = (bf16[16,24,128]{2,1,0:T(8,128)(2,1)S(1)}, bf16[16,24,128]{2,1,0:T(8,128)(2,1)S(1)}, u32[]{:S(2)}, u32[]{:S(2)}) collective-permute-start(bf16[16,24,128]{2,1,0:T(8,128)(2,1)S(1)} %get-tuple-element.31.high), channel_id=1, source_target_pairs={{0,7},{1,2},{2,1},{3,4},{4,3},{5,6},{6,5},{7,0},{8,15},{9,10},{10,... | collective-permute-start | bytes 294920 | tf_op jit(solution)/shard_map/ppermute | solution.py:41
  41.2 5.6 %collective-permute-start.10 = (bf16[16,24,128]{2,1,0:T(8,128)(2,1)S(1)}, bf16[16,24,128]{2,1,0:T(8,128)(2,1)S(1)}, u32[]{:S(2)}, u32[]{:S(2)}) collective-permute-start(bf16[16,24,128]{2,1,0:T(8,128)(2,1)S(1)} %get-tuple-element.31.high), channel_id=1, source_target_pairs={{0,1},{1,0},{2,3},{3,2},{4,5},{5,4},{6,7},{7,6},{8,9},{9,8},{10,11... | collective-permute-start | bytes 294920 | tf_op jit(solution)/shard_map/ppermute | solution.py:41
  41.2 5.6 %collective-permute-start.9 = (bf16[16,24,128]{2,1,0:T(8,128)(2,1)S(1)}, bf16[16,24,128]{2,1,0:T(8,128)(2,1)S(1)}, u32[]{:S(2)}, u32[]{:S(2)}) collective-permute-start(bf16[16,24,128]{2,1,0:T(8,128)(2,1)S(1)} %get-tuple-element.31.high), channel_id=1, source_target_pairs={{0,24},{8,16},{16,8},{24,0},{1,25},{9,17},{17,9},{25,1},{2,26},{10... | collective-permute-start | bytes 294920 | tf_op jit(solution)/shard_map/ppermute | solution.py:41
  41.2 5.6 %collective-permute-start.8 = (bf16[16,24,128]{2,1,0:T(8,128)(2,1)S(1)}, bf16[16,24,128]{2,1,0:T(8,128)(2,1)S(1)}, u32[]{:S(2)}, u32[]{:S(2)}) collective-permute-start(bf16[16,24,128]{2,1,0:T(8,128)(2,1)S(1)} %get-tuple-element.31.high), channel_id=1, source_target_pairs={{0,8},{8,0},{16,24},{24,16},{1,9},{9,1},{17,25},{25,17},{2,10},{10... | collective-permute-start | bytes 294920 | tf_op jit(solution)/shard_map/ppermute | solution.py:41
where the time goes:
time: 63.3 us; the launch traced here: 63.1 us
  Pallas kernels  23.5 us (37%)
  starting transfers between devices  13.9 us (22%)
  blocking collectives  10.6 us (17%)
  waiting for transfers between devices  9.09 us (14%)
  local copies, waits for them, and re-layouts  5.14 us (8%)
  between operations  0.75 us (1%)
    ppermute x6, starting transfers between devices, exchange(): lax.ppermute(high, axis, second)  11.5 us
    all_to_all x1, blocking collectives, on_device(): sums = lax.all_to_all(sums, ('grp', 'dev'), 0, 0)  10.6 us
    pallas_call x1, Pallas kernels, on_device(): pl.pallas_call(functools.partial(first_local_kernel, dims), in_specs=[VM,...  7.94 us
    pallas_call x1, Pallas kernels, restrict(): pl.pallas_call(restrict_kernel, in_specs=[ANY, ANY], out_specs=[VM] * 4,...  7.21 us
    ppermute x6, waiting for transfers between devices, exchange(): lax.ppermute(high, axis, second)  7.19 us
    unnamed x10, local copies, waits for them, and re-layouts  5.14 us
    pallas_call x1, Pallas kernels, on_device(): pl.pallas_call(finish_kernel, in_specs=[VM] * 8, out_specs=[ANY, VM], out...  4.64 us
    ppermute x6, starting transfers between devices, exchange(): lax.ppermute(high, axis, first)  2.45 us
  transfers between devices with their start and end apart: 12, of which 4 were waited for; matrix products, arithmetic and copies ran while one was open for 0% of the time, Pallas kernels for 15%

commit v1 on v0

--- a/solution.py
+++ b/solution.py
@@ -9,13 +9,14 @@
 
 ITERS = 3
 SHIFT = 3.0
-LIMIT = 40 * 1024 * 1024
+EACH = 2
+LIMIT = 16 * 1024 * 1024
 F32 = jnp.float32
 BF16 = jnp.bfloat16
 NT = (((1,), (1,)), ((), ()))
 NN = (((1,), (0,)), ((), ()))
 VM = pl.BlockSpec(memory_space=pltpu.VMEM)
-ANY = pl.BlockSpec(memory_space=pl.ANY)
+HBM = pl.BlockSpec(memory_space=pltpu.HBM)
 PARAMS = pltpu.CompilerParams(vmem_limit_bytes=LIMIT)
 
 
@@ -63,23 +64,30 @@
     return jnp.concatenate([product[:rows], product[rows:]], axis=1)
 
 
-def restrict_kernel(field_hbm, near_hbm, source_ref, high_ref, low_ref, near_ref, field, prods, sem):
-    sites = field.shape[0]
-    nrhs = field.shape[1]
+def restrict_kernel(
+    field_hbm, near_hbm, oper_hbm, source_ref, high_ref, low_ref, near_ref, oper_ref, field, prods, sem, oper_sem
+):
+    sites, nrhs = field.shape[:2]
     middle = field.shape[-1] // 2
+    nvec = near_ref.shape[1] // 2
+    wide = 4 * nvec
+    groups = sem.shape[1]
+    each = EACH
     copies = []
-    for s in range(sites):
+    for g in range(groups):
+        span = pl.ds(g * each, each)
         pair = (
-            pltpu.make_async_copy(field_hbm.at[s], field.at[s], sem.at[0, s]),
-            pltpu.make_async_copy(near_hbm.at[s], near_ref.at[s], sem.at[1, s]),
+            pltpu.make_async_copy(field_hbm.at[span], field.at[span], sem.at[0, g]),
+            pltpu.make_async_copy(near_hbm.at[span], near_ref.at[span], sem.at[1, g]),
         )
         for copy in pair:
             copy.start()
         copies.append(pair)
-    nvec = near_ref.shape[1] // 2
-    for s in range(sites):
-        for copy in copies[s]:
-            copy.wait()
+    last = pltpu.make_async_copy(oper_hbm.at[lax.axis_index("grp")], oper_ref, oper_sem)
+    last.start()
+    lane = lanes((nrhs, wide))
+
+    def multiply(s):
         fine = field[s].reshape(2 * nrhs, 2 * middle)
         near = near_ref[s]
         parts = [
@@ -92,13 +100,12 @@
             for h in range(2)
         ]
         prods[s] = jnp.concatenate(parts, axis=1)
-    for s in range(sites):
+
+    def arrange(s):
         even = prods[s, pl.ds(0, nrhs, 2), :]
         odd = prods[s, pl.ds(1, nrhs, 2), :]
-        wide = 4 * nvec
         real = even + pltpu.roll(odd, wide - nvec, 1)
         imag = odd - pltpu.roll(even, wide - nvec, 1)
-        lane = lanes(real.shape)
         value = jnp.where(
             lane < nvec,
             real,
@@ -109,32 +116,43 @@
             ),
         )
         source_ref[s] = value
-        high, low = halves(value)
-        high_ref[s] = high
-        low_ref[s] = low
-
-
-def restrict(field, near):
+        high_ref[s], low_ref[s] = halves(value)
+
+    for g in range(groups + 1):
+        if g < groups:
+            for copy in copies[g]:
+                copy.wait()
+            for s in range(g * each, (g + 1) * each):
+                multiply(s)
+        if g:
+            for s in range((g - 1) * each, g * each):
+                arrange(s)
+    last.wait()
+
+
+def restrict(field, near, oper):
     sites, nrhs, _, fine = field.shape
     coarse = 2 * near.shape[1]
     return pl.pallas_call(
         restrict_kernel,
-        in_specs=[ANY, ANY],
-        out_specs=[VM] * 4,
+        in_specs=[HBM] * 3,
+        out_specs=[VM] * 5,
         out_shape=[
             jax.ShapeDtypeStruct((sites, nrhs, coarse), F32),
             jax.ShapeDtypeStruct((sites, nrhs, coarse), BF16),
             jax.ShapeDtypeStruct((sites, nrhs, coarse), BF16),
             jax.ShapeDtypeStruct(near.shape, BF16),
+            jax.ShapeDtypeStruct(oper.shape[1:], BF16),
         ],
         scratch_shapes=[
             pltpu.VMEM(field.shape, BF16),
             pltpu.VMEM((sites, 2 * nrhs, coarse), F32),
-            pltpu.SemaphoreType.DMA((2, sites)),
+            pltpu.SemaphoreType.DMA((2, sites // EACH)),
+            pltpu.SemaphoreType.DMA,
         ],
         compiler_params=PARAMS,
         name="restrict",
-    )(field, near)
+    )(field, near, oper)
 
 
 def neighbours(s, ly, lx):
@@ -161,19 +179,12 @@
     return total, [centre[(i + 1) * rows : (i + 2) * rows] for i in range(len(extra))]
 
 
-def first_local_kernel(dims, high, low, oper_hbm, part_ref, rest_ref, oper_ref, xy, sem):
+def first_local_kernel(dims, high, low, oper_ref, part_ref, rest_ref, xy):
     sites = xy.shape[0]
-    copies = []
-    plane = lax.axis_index("grp")
-    for s in range(sites):
-        copy = pltpu.make_async_copy(oper_hbm.at[plane, s], oper_ref.at[s], sem.at[s])
-        copy.start()
-        copies.append(copy)
+    rows = high.shape[1]
     for s in range(sites):
         xy[s] = stacked(high[s])
-    rows = high.shape[1]
     for s in range(sites):
-        copies[s].wait()
         total, extra = local_product(s, dims, oper_ref[s], xy, [low[s]])
         part_ref[s] = joined(total, rows)
         rest_ref[s] = joined(extra[0], rows)
@@ -354,7 +365,7 @@
     return answer, residual
 
 
-def finish_kernel(sums, r0, v1, w1, v2, w2, v3, near, fine_hbm, resid_ref, coef, fine, sem):
+def finish_kernel(sums, r0, v1, w1, v2, w2, v3, near, fine_hbm, resid_hbm, coef, mixed, fine, resid, sem, resid_sem):
     sites, rows, wide = r0.shape
     half = wide // 2
     quarter = half // 2
@@ -388,31 +399,68 @@
         for e, (which, index, _) in enumerate(entries)
     ]
     lane = lanes((rows, wide))
-    copies = []
-    for s in range(sites):
+    def combined(s):
         plain = [b[s] for b in basis]
         rolled = [pltpu.roll(p, half, 1) for p in plain]
         out = [jnp.zeros((rows, wide), F32), jnp.zeros((rows, wide), F32)]
         for which, index, re, im in spread:
             out[which] = out[which] + re * plain[index] + im * rolled[index]
-        resid_ref[s] = out[1]
+        resid[s] = out[1]
         x = out[0].astype(BF16).astype(F32)
         by1 = pltpu.roll(x, wide - quarter, 1)
         by2 = pltpu.roll(x, half, 1)
         by3 = pltpu.roll(x, quarter, 1)
-        upper = (jnp.where(lane < quarter, x, -by1), jnp.where(lane < quarter, by2, by3))
-        lower = (jnp.where(lane < quarter, by1, -by2), jnp.where(lane < quarter, by3, x))
-        for h, (first, second) in enumerate((upper, lower)):
-            mixed = jnp.stack([first, second], axis=1).reshape(2 * rows, wide)[:, :half].astype(BF16)
+        mixed[s, 0, pl.ds(0, rows, 2), :] = jnp.where(lane < quarter, x, -by1)
+        mixed[s, 0, pl.ds(1, rows, 2), :] = jnp.where(lane < quarter, by2, by3)
+        mixed[s, 1, pl.ds(0, rows, 2), :] = jnp.where(lane < quarter, by1, -by2)
+        mixed[s, 1, pl.ds(1, rows, 2), :] = jnp.where(lane < quarter, by3, x)
+
+    def prolonged(s):
+        for h in range(2):
+            cols = slice(h * middle, (h + 1) * middle)
             product = lax.dot_general(
-                mixed, near[s, :, h * middle : (h + 1) * middle], NN, preferred_element_type=F32
+                mixed[s, h, :, :half].astype(BF16), near[s, :, cols], NN, preferred_element_type=F32
             )
-            fine[s, :, :, h * middle : (h + 1) * middle] = product.astype(BF16).reshape(rows, 2, middle)
-        copy = pltpu.make_async_copy(fine.at[s], fine_hbm.at[s], sem.at[s])
-        copy.start()
-        copies.append(copy)
+            fine[s, :, :, cols] = product.astype(BF16).reshape(rows, 2, middle)
+
+    groups = sem.shape[0]
+    copies = []
+    for g in range(groups + 1):
+        if g < groups:
+            for s in range(g * EACH, (g + 1) * EACH):
+                combined(s)
+        if g == groups - 1:
+            copies.append(pltpu.make_async_copy(resid, resid_hbm, resid_sem))
+            copies[-1].start()
+        if g:
+            span = pl.ds((g - 1) * EACH, EACH)
+            for s in range((g - 1) * EACH, g * EACH):
+                prolonged(s)
+            copies.append(pltpu.make_async_copy(fine.at[span], fine_hbm.at[span], sem.at[g - 1]))
+            copies[-1].start()
     for copy in copies:
         copy.wait()
+
+
+def finish(sums, *arrays):
+    sites, nrhs, wide = arrays[0].shape
+    fine = (sites, nrhs, 2, arrays[-1].shape[-1])
+    return pl.pallas_call(
+        finish_kernel,
+        in_specs=[VM] * 8,
+        out_specs=[HBM, HBM],
+        out_shape=[jax.ShapeDtypeStruct(fine, BF16), jax.ShapeDtypeStruct((sites, nrhs, wide), F32)],
+        scratch_shapes=[
+            pltpu.VMEM((wide, wide), F32),
+            pltpu.VMEM((sites, 2, 2 * nrhs, wide), F32),
+            pltpu.VMEM(fine, BF16),
+            pltpu.VMEM((sites, nrhs, wide), F32),
+            pltpu.SemaphoreType.DMA((sites // EACH,)),
+            pltpu.SemaphoreType.DMA,
+        ],
+        compiler_params=PARAMS,
+        name="finish",
+    )(sums, *arrays)
 
 
 def on_device(fine_residual, near_null, coarse_operator):
@@ -424,19 +472,20 @@
     near = near_null.reshape(sites, 2 * nvec, fine)
     oper = coarse_operator.reshape((-1, sites) + coarse_operator.shape[-2:])
     dims = (ly, lx)
+    field, near, oper = (pltpu.with_memory_space_constraint(a, pltpu.HBM) for a in (field, near, oper))
     vector = jax.ShapeDtypeStruct((sites, nrhs, wide), F32)
     rounded = jax.ShapeDtypeStruct((sites, nrhs, wide), BF16)
     xy = pltpu.VMEM((sites, 2 * nrhs, wide), BF16)
 
-    r0, h0, l0, near = restrict(field, near)
+    r0, h0, l0, near, oper = restrict(field, near, oper)
 
     planes = exchange(h0)
-    part, w1, oper = pl.pallas_call(
+    part, w1 = pl.pallas_call(
         functools.partial(first_local_kernel, dims),
-        in_specs=[VM, VM, ANY],
-        out_specs=[VM] * 3,
-        out_shape=[vector, vector, jax.ShapeDtypeStruct(oper.shape[1:], BF16)],
-        scratch_shapes=[xy, pltpu.SemaphoreType.DMA((sites,))],
+        in_specs=[VM] * 3,
+        out_specs=[VM] * 2,
+        out_shape=[vector, vector],
+        scratch_shapes=[xy],
         compiler_params=PARAMS,
         name="local_1",
     )(h0, l0, oper)
@@ -489,19 +538,7 @@
     )(*planes, part, r0, v1, w1, v2, w2, oper)
 
     sums = lax.all_to_all(sums, ("grp", "dev"), 0, 0)
-    correction, residual = pl.pallas_call(
-        finish_kernel,
-        in_specs=[VM] * 8,
-        out_specs=[ANY, VM],
-        out_shape=[jax.ShapeDtypeStruct(field.shape, BF16), vector],
-        scratch_shapes=[
-            pltpu.VMEM((wide, wide), F32),
-            pltpu.VMEM(field.shape, BF16),
-            pltpu.SemaphoreType.DMA((sites,)),
-        ],
-        compiler_params=PARAMS,
-        name="finish",
-    )(sums, r0, v1, w1, v2, w2, v3, near)
+    correction, residual = finish(sums, r0, v1, w1, v2, w2, v3, near)
     return correction.reshape(fine_residual.shape), residual.reshape((1, 1, ly, lx, nrhs, wide))
 
 

time: 63.3 us -> 50.5 us (0.80)
  Pallas kernels: 23.5 us -> 13.1 us
  local copies, waits for them, and re-layouts: 5.14 us -> 0 us
  waiting for transfers between devices: 9.09 us -> 10.7 us
  starting transfers between devices: 13.9 us -> 15.2 us
    pallas_call x3, Pallas kernels: 19.8 us -> 9.36 us  [the longest x1 5.07 us: restrict(): pl.pallas_call(restrict_kernel, in_specs=[HBM] * 3, out_specs=[VM] * 5, o...]
    unnamed x10 -> x0, local copies, waits for them, and re-layouts: 5.14 us -> none
    ppermute x6, waiting for transfers between devices: 1.91 us -> 4 us  [exchange(): lax.ppermute(high, axis, first)]
    ppermute x6, starting transfers between devices: 2.45 us -> 3.34 us  [exchange(): lax.ppermute(high, axis, first)]
  transfers between devices with their start and end apart: 12 -> 12, of which waited for: 4 -> 7; matrix products, arithmetic and copies ran while one was open for 0% -> 0% of each run, Pallas kernels for 15% -> 4%
where the time goes in v1:
time: 50.5 us; the launch traced here: 50.3 us
  starting transfers between devices  15.2 us (30%)
  Pallas kernels  13.1 us (26%)
  waiting for transfers between devices  10.7 us (21%)
  blocking collectives  10.6 us (21%)
  between operations  0.68 us (1%)
    ppermute x6, starting transfers between devices, exchange(): lax.ppermute(high, axis, second)  11.9 us
    all_to_all x1, blocking collectives, on_device(): sums = lax.all_to_all(sums, ('grp', 'dev'), 0, 0)  10.6 us
    ppermute x6, waiting for transfers between devices, exchange(): lax.ppermute(high, axis, second)  6.75 us
    pallas_call x1, Pallas kernels, restrict(): pl.pallas_call(restrict_kernel, in_specs=[HBM] * 3, out_specs=[VM] * 5, o...  5.07 us
    ppermute x6, waiting for transfers between devices, exchange(): lax.ppermute(high, axis, first)  4 us
    pallas_call x1, Pallas kernels, finish(): pl.pallas_call(finish_kernel, in_specs=[VM] * 8, out_specs=[HBM, HBM], ou...  3.6 us
    ppermute x6, starting transfers between devices, exchange(): lax.ppermute(high, axis, first)  3.34 us
    pallas_call x2, Pallas kernels, on_device(): pl.pallas_call(halo_kernel, in_specs=[VM] * 7, out_specs=[VM] * 3, out_sh...  1.11 us
  transfers between devices with their start and end apart: 12, of which 7 were waited for; matrix products, arithmetic and copies ran while one was open for 0% of the time, Pallas kernels for 4%

profile of v1, /device:TPU:0, one launch (start us, length us, event | category | flops | bytes accessed | tf_op | source)
XLA Modules:
  0.0 50.3 jit_solution(16499639022771180167)
XLA Ops:
  0.6 5.1 %restrict.1 = (f32[16,24,128]{2,1,0:T(8,128)S(1)}, bf16[16,24,128]{2,1,0:T(8,128)(2,1)S(1)}, bf16[16,24,128]{2,1,0:T(8,128)(2,1)S(1)}, bf16[16,64,3072]{2,1,0:T(8,128)(2,1)S(1)}, bf16[16,64,1152]{2,1,0:T(8,128)(2,1)S(1)}) custom-call(bf16[16,24,2,3072]{3,2,1,0:T(2,128)(2,1)} %bitcast.7, bf16[16,64,3072]{2,1,0:T(8,128)(2,1)} %bitcast.6, ...), custom_call_target="tpu_custom_call" | custom-call | tf_op jit(solution)/shard_map/restrict/pallas_call | solution.py:136
  5.7 6.1 %collective-permute-start.3 = (bf16[16,24,128]{2,1,0:T(8,128)(2,1)S(1)}, bf16[16,24,128]{2,1,0:T(8,128)(2,1)S(1)}, u32[]{:S(2)}, u32[]{:S(2)}) collective-permute-start(bf16[16,24,128]{2,1,0:T(8,128)(2,1)S(1)} %get-tuple-element.21.high), channel_id=1, source_target_pairs={{0,7},{1,2},{2,1},{3,4},{4,3},{5,6},{6,5},{7,0},{8,15},{9,10},{10,... | collective-permute-start | bytes 294920 | tf_op jit(solution)/shard_map/ppermute | solution.py:42
  11.8 0.0 collective-permute-start.2
  11.8 0.7 %collective-permute-start.1 = (bf16[16,24,128]{2,1,0:T(8,128)(2,1)S(1)}, bf16[16,24,128]{2,1,0:T(8,128)(2,1)S(1)}, u32[]{:S(2)}, u32[]{:S(2)}) collective-permute-start(bf16[16,24,128]{2,1,0:T(8,128)(2,1)S(1)} %get-tuple-element.21.high), channel_id=1, source_target_pairs={{0,24},{8,16},{16,8},{24,0},{1,25},{9,17},{17,9},{25,1},{2,26},{10... | collective-permute-start | bytes 294920 | tf_op jit(solution)/shard_map/ppermute | solution.py:42
  12.4 1.0 %collective-permute-start = (bf16[16,24,128]{2,1,0:T(8,128)(2,1)S(1)}, bf16[16,24,128]{2,1,0:T(8,128)(2,1)S(1)}, u32[]{:S(2)}, u32[]{:S(2)}) collective-permute-start(bf16[16,24,128]{2,1,0:T(8,128)(2,1)S(1)} %get-tuple-element.21.high), channel_id=1, source_target_pairs={{0,8},{8,0},{16,24},{24,16},{1,9},{9,1},{17,25},{25,17},{2,10},{10... | collective-permute-start | bytes 294920 | tf_op jit(solution)/shard_map/ppermute | solution.py:42
  13.4 0.7 %local_1.1 = (f32[16,24,128]{2,1,0:T(8,128)S(1)}, f32[16,24,128]{2,1,0:T(8,128)S(1)}) custom-call(bf16[16,24,128]{2,1,0:T(8,128)(2,1)S(1)} %get-tuple-element.21.high, bf16[16,24,128]{2,1,0:T(8,128)(2,1)S(1)} %get-tuple-element.22.low, bf16[16,64,1152]{2,1,0:T(8,128)(2,1)S(1)} %get-tuple-element.23.oper_ref.refs_1_.refs_0_), custom_call_target="tpu_custom_call" | custom-call | tf_op jit(solution)/shard_map/local_1/pallas_call | solution.py:483
  14.1 0.6 %collective-permute-done.3.z_two = bf16[16,24,128]{2,1,0:T(8,128)(2,1)S(1)} collective-permute-done((bf16[16,24,128]{2,1,0:T(8,128)(2,1)S(1)}, bf16[16,24,128]{2,1,0:T(8,128)(2,1)S(1)}, u32[]{:S(2)}, u32[]{:S(2)}) %collective-permute-start.3) | collective-permute-done | bytes 98336 | tf_op jit(solution)/shard_map/ppermute | solution.py:42
  14.6 2.0 %collective-permute-done.2.z_one = bf16[16,24,128]{2,1,0:T(8,128)(2,1)S(1)} collective-permute-done((bf16[16,24,128]{2,1,0:T(8,128)(2,1)S(1)}, bf16[16,24,128]{2,1,0:T(8,128)(2,1)S(1)}, u32[]{:S(2)}, u32[]{:S(2)}) %collective-permute-start.2) | collective-permute-done | bytes 98336 | tf_op jit(solution)/shard_map/ppermute | solution.py:42
  16.7 0.2 collective-permute-done.1.t_two
  16.8 0.6 %halo_1.1 = (f32[16,24,128]{2,1,0:T(8,128)S(1)}, bf16[16,24,128]{2,1,0:T(8,128)(2,1)S(1)}, bf16[16,24,128]{2,1,0:T(8,128)(2,1)S(1)}) custom-call(bf16[16,24,128]{2,1,0:T(8,128)(2,1)S(1)} %collective-permute-done.t_one, bf16[16,24,128]{2,1,0:T(8,128)(2,1)S(1)} %collective-permute-done.1.t_two, bf16[16,24,128]{2,1,0:T(8,128)(2,1)S(1)} %collective-permute-done.2.z_one, ...), custom_call_target="tpu_custom_call" | custom-call | tf_op jit(solution)/shard_map/halo_1/pallas_call | solution.py:492
  17.4 2.3 %collective-permute-start.7 = (bf16[16,24,128]{2,1,0:T(8,128)(2,1)S(1)}, bf16[16,24,128]{2,1,0:T(8,128)(2,1)S(1)}, u32[]{:S(2)}, u32[]{:S(2)}) collective-permute-start(bf16[16,24,128]{2,1,0:T(8,128)(2,1)S(1)} %get-tuple-element.26.high), channel_id=1, source_target_pairs={{0,7},{1,2},{2,1},{3,4},{4,3},{5,6},{6,5},{7,0},{8,15},{9,10},{10,... | collective-permute-start | bytes 294920 | tf_op jit(solution)/shard_map/ppermute | solution.py:42
  19.7 1.6 %collective-permute-start.4 = (bf16[16,24,128]{2,1,0:T(8,128)(2,1)S(1)}, bf16[16,24,128]{2,1,0:T(8,128)(2,1)S(1)}, u32[]{:S(2)}, u32[]{:S(2)}) collective-permute-start(bf16[16,24,128]{2,1,0:T(8,128)(2,1)S(1)} %get-tuple-element.26.high), channel_id=1, source_target_pairs={{0,8},{8,0},{16,24},{24,16},{1,9},{9,1},{17,25},{25,17},{2,10},{10... | collective-permute-start | bytes 294920 | tf_op jit(solution)/shard_map/ppermute | solution.py:42
  21.3 0.9 %local_2.1 = (f32[16,24,128]{2,1,0:T(8,128)S(1)}, f32[16,24,128]{2,1,0:T(8,128)S(1)}) custom-call(bf16[16,24,128]{2,1,0:T(8,128)(2,1)S(1)} %get-tuple-element.26.high, bf16[16,24,128]{2,1,0:T(8,128)(2,1)S(1)} %get-tuple-element.27.low, f32[16,24,128]{2,1,0:T(8,128)S(1)} %get-tuple-element.28.refs_0_.w1, ...), custom_call_target="tpu_custom_call" | custom-call | tf_op jit(solution)/shard_map/local_2/pallas_call | solution.py:502
  22.2 2.9 %collective-permute-done.7.z_two = bf16[16,24,128]{2,1,0:T(8,128)(2,1)S(1)} collective-permute-done((bf16[16,24,128]{2,1,0:T(8,128)(2,1)S(1)}, bf16[16,24,128]{2,1,0:T(8,128)(2,1)S(1)}, u32[]{:S(2)}, u32[]{:S(2)}) %collective-permute-start.7) | collective-permute-done | bytes 98336 | tf_op jit(solution)/shard_map/ppermute | solution.py:42
  25.1 1.0 %collective-permute-done.6.z_one = bf16[16,24,128]{2,1,0:T(8,128)(2,1)S(1)} collective-permute-done((bf16[16,24,128]{2,1,0:T(8,128)(2,1)S(1)}, bf16[16,24,128]{2,1,0:T(8,128)(2,1)S(1)}, u32[]{:S(2)}, u32[]{:S(2)}) %collective-permute-start.6) | collective-permute-done | bytes 98336 | tf_op jit(solution)/shard_map/ppermute | solution.py:42
  26.1 0.6 %halo_2.1 = (f32[16,24,128]{2,1,0:T(8,128)S(1)}, bf16[16,24,128]{2,1,0:T(8,128)(2,1)S(1)}, bf16[16,24,128]{2,1,0:T(8,128)(2,1)S(1)}) custom-call(bf16[16,24,128]{2,1,0:T(8,128)(2,1)S(1)} %collective-permute-done.4.t_one, bf16[16,24,128]{2,1,0:T(8,128)(2,1)S(1)} %collective-permute-done.5.t_two, bf16[16,24,128]{2,1,0:T(8,128)(2,1)S(1)} %collective-permute-done.6.z_one, ...), custom_call_target="tpu_custom_call" | custom-call | tf_op jit(solution)/shard_map/halo_2/pallas_call | solution.py:511
  26.6 2.8 %collective-permute-start.11 = (bf16[16,24,128]{2,1,0:T(8,128)(2,1)S(1)}, bf16[16,24,128]{2,1,0:T(8,128)(2,1)S(1)}, u32[]{:S(2)}, u32[]{:S(2)}) collective-permute-start(bf16[16,24,128]{2,1,0:T(8,128)(2,1)S(1)} %get-tuple-element.31.high), channel_id=1, source_target_pairs={{0,7},{1,2},{2,1},{3,4},{4,3},{5,6},{6,5},{7,0},{8,15},{9,10},{10,... | collective-permute-start | bytes 294920 | tf_op jit(solution)/shard_map/ppermute | solution.py:42
  29.5 0.8 %collective-permute-start.8 = (bf16[16,24,128]{2,1,0:T(8,128)(2,1)S(1)}, bf16[16,24,128]{2,1,0:T(8,128)(2,1)S(1)}, u32[]{:S(2)}, u32[]{:S(2)}) collective-permute-start(bf16[16,24,128]{2,1,0:T(8,128)(2,1)S(1)} %get-tuple-element.31.high), channel_id=1, source_target_pairs={{0,8},{8,0},{16,24},{24,16},{1,9},{9,1},{17,25},{25,17},{2,10},{10... | collective-permute-start | bytes 294920 | tf_op jit(solution)/shard_map/ppermute | solution.py:42
  30.2 0.7 %local_3.1.part = f32[16,24,128]{2,1,0:T(8,128)S(1)} custom-call(bf16[16,24,128]{2,1,0:T(8,128)(2,1)S(1)} %get-tuple-element.31.high, bf16[16,24,128]{2,1,0:T(8,128)(2,1)S(1)} %get-tuple-element.32.low, bf16[16,64,1152]{2,1,0:T(8,128)(2,1)S(1)} %get-tuple-element.23.oper_ref.refs_1_.refs_0_), custom_call_target="tpu_custom_call" | custom-call | tf_op jit(solution)/shard_map/local_3/pallas_call | solution.py:521
  30.9 3.2 %collective-permute-done.11.z_two = bf16[16,24,128]{2,1,0:T(8,128)(2,1)S(1)} collective-permute-done((bf16[16,24,128]{2,1,0:T(8,128)(2,1)S(1)}, bf16[16,24,128]{2,1,0:T(8,128)(2,1)S(1)}, u32[]{:S(2)}, u32[]{:S(2)}) %collective-permute-start.11) | collective-permute-done | bytes 98336 | tf_op jit(solution)/shard_map/ppermute | solution.py:42
  34.1 1.0 %collective-permute-done.10.z_one = bf16[16,24,128]{2,1,0:T(8,128)(2,1)S(1)} collective-permute-done((bf16[16,24,128]{2,1,0:T(8,128)(2,1)S(1)}, bf16[16,24,128]{2,1,0:T(8,128)(2,1)S(1)}, u32[]{:S(2)}, u32[]{:S(2)}) %collective-permute-start.10) | collective-permute-done | bytes 98336 | tf_op jit(solution)/shard_map/ppermute | solution.py:42
  35.1 1.1 %halo_3.1 = (f32[16,24,128]{2,1,0:T(8,128)S(1)}, f32[32,8,128]{2,1,0:T(8,128)S(1)}) custom-call(bf16[16,24,128]{2,1,0:T(8,128)(2,1)S(1)} %collective-permute-done.8.t_one, bf16[16,24,128]{2,1,0:T(8,128)(2,1)S(1)} %collective-permute-done.9.t_two, bf16[16,24,128]{2,1,0:T(8,128)(2,1)S(1)} %collective-permute-done.10.z_one, ...), custom_call_target="tpu_custom_call" | custom-call | tf_op jit(solution)/shard_map/halo_3/pallas_call | solution.py:531
  36.2 10.6 %all_to_all.5.sums = f32[32,8,128]{2,1,0:T(8,128)S(1)} all-to-all(f32[32,8,128]{2,1,0:T(8,128)S(1)} %get-tuple-element.35), channel_id=1, replica_groups=mesh['grp'=4,'dev'=8] {'grp','dev'}, dimensions={0} | all-to-all | bytes 262144 | tf_op jit(solution)/shard_map/all_to_all | solution.py:540
  46.7 3.6 %finish.1 = (bf16[16,24,2,3072]{3,2,1,0:T(2,128)(2,1)}, f32[16,24,128]{2,1,0:T(8,128)}) custom-call(f32[32,8,128]{2,1,0:T(8,128)S(1)} %all_to_all.5.sums, f32[16,24,128]{2,1,0:T(8,128)S(1)} %get-tuple-element.25.before.r0, f32[16,24,128]{2,1,0:T(8,128)S(1)} %get-tuple-element.30.before.v1, f32[16,24,128]{2,1,0:T(8,128)S(1)} %get-tuple-element.28.refs_0_.w1, ...), custom_call_target="tpu_custom_call" | custom-call | tf_op jit(solution)/shard_map/finish/pallas_call | solution.py:448
  (9 shorter events, 0.0 us)
Async XLA Ops:
  5.7 8.9 %collective-permute-start.3 = (bf16[16,24,128]{2,1,0:T(8,128)(2,1)S(1)}, bf16[16,24,128]{2,1,0:T(8,128)(2,1)S(1)}, u32[]{:S(2)}, u32[]{:S(2)}) collective-permute-start(bf16[16,24,128]{2,1,0:T(8,128)(2,1)S(1)} %get-tuple-element.21.high), channel_id=1, source_target_pairs={{0,7},{1,2},{2,1},{3,4},{4,3},{5,6},{6,5},{7,0},{8,15},{9,10},{10,... | collective-permute-start | bytes 294920 | tf_op jit(solution)/shard_map/ppermute | solution.py:42
  11.8 4.9 %collective-permute-start.2 = (bf16[16,24,128]{2,1,0:T(8,128)(2,1)S(1)}, bf16[16,24,128]{2,1,0:T(8,128)(2,1)S(1)}, u32[]{:S(2)}, u32[]{:S(2)}) collective-permute-start(bf16[16,24,128]{2,1,0:T(8,128)(2,1)S(1)} %get-tuple-element.21.high), channel_id=1, source_target_pairs={{0,1},{1,0},{2,3},{3,2},{4,5},{5,4},{6,7},{7,6},{8,9},{9,8},{10,11... | collective-permute-start | bytes 294920 | tf_op jit(solution)/shard_map/ppermute | solution.py:42
  11.8 5.1 %collective-permute-start.1 = (bf16[16,24,128]{2,1,0:T(8,128)(2,1)S(1)}, bf16[16,24,128]{2,1,0:T(8,128)(2,1)S(1)}, u32[]{:S(2)}, u32[]{:S(2)}) collective-permute-start(bf16[16,24,128]{2,1,0:T(8,128)(2,1)S(1)} %get-tuple-element.21.high), channel_id=1, source_target_pairs={{0,24},{8,16},{16,8},{24,0},{1,25},{9,17},{17,9},{25,1},{2,26},{10... | collective-permute-start | bytes 294920 | tf_op jit(solution)/shard_map/ppermute | solution.py:42
  12.4 4.4 %collective-permute-start = (bf16[16,24,128]{2,1,0:T(8,128)(2,1)S(1)}, bf16[16,24,128]{2,1,0:T(8,128)(2,1)S(1)}, u32[]{:S(2)}, u32[]{:S(2)}) collective-permute-start(bf16[16,24,128]{2,1,0:T(8,128)(2,1)S(1)} %get-tuple-element.21.high), channel_id=1, source_target_pairs={{0,8},{8,0},{16,24},{24,16},{1,9},{9,1},{17,25},{25,17},{2,10},{10... | collective-permute-start | bytes 294920 | tf_op jit(solution)/shard_map/ppermute | solution.py:42
  17.4 7.7 %collective-permute-start.7 = (bf16[16,24,128]{2,1,0:T(8,128)(2,1)S(1)}, bf16[16,24,128]{2,1,0:T(8,128)(2,1)S(1)}, u32[]{:S(2)}, u32[]{:S(2)}) collective-permute-start(bf16[16,24,128]{2,1,0:T(8,128)(2,1)S(1)} %get-tuple-element.26.high), channel_id=1, source_target_pairs={{0,7},{1,2},{2,1},{3,4},{4,3},{5,6},{6,5},{7,0},{8,15},{9,10},{10,... | collective-permute-start | bytes 294920 | tf_op jit(solution)/shard_map/ppermute | solution.py:42
  19.7 6.3 %collective-permute-start.6 = (bf16[16,24,128]{2,1,0:T(8,128)(2,1)S(1)}, bf16[16,24,128]{2,1,0:T(8,128)(2,1)S(1)}, u32[]{:S(2)}, u32[]{:S(2)}) collective-permute-start(bf16[16,24,128]{2,1,0:T(8,128)(2,1)S(1)} %get-tuple-element.26.high), channel_id=1, source_target_pairs={{0,1},{1,0},{2,3},{3,2},{4,5},{5,4},{6,7},{7,6},{8,9},{9,8},{10,11... | collective-permute-start | bytes 294920 | tf_op jit(solution)/shard_map/ppermute | solution.py:42
  19.7 6.3 %collective-permute-start.5 = (bf16[16,24,128]{2,1,0:T(8,128)(2,1)S(1)}, bf16[16,24,128]{2,1,0:T(8,128)(2,1)S(1)}, u32[]{:S(2)}, u32[]{:S(2)}) collective-permute-start(bf16[16,24,128]{2,1,0:T(8,128)(2,1)S(1)} %get-tuple-element.26.high), channel_id=1, source_target_pairs={{0,24},{8,16},{16,8},{24,0},{1,25},{9,17},{17,9},{25,1},{2,26},{10... | collective-permute-start | bytes 294920 | tf_op jit(solution)/shard_map/ppermute | solution.py:42
  19.7 6.3 %collective-permute-start.4 = (bf16[16,24,128]{2,1,0:T(8,128)(2,1)S(1)}, bf16[16,24,128]{2,1,0:T(8,128)(2,1)S(1)}, u32[]{:S(2)}, u32[]{:S(2)}) collective-permute-start(bf16[16,24,128]{2,1,0:T(8,128)(2,1)S(1)} %get-tuple-element.26.high), channel_id=1, source_target_pairs={{0,8},{8,0},{16,24},{24,16},{1,9},{9,1},{17,25},{25,17},{2,10},{10... | collective-permute-start | bytes 294920 | tf_op jit(solution)/shard_map/ppermute | solution.py:42
  26.6 7.5 %collective-permute-start.11 = (bf16[16,24,128]{2,1,0:T(8,128)(2,1)S(1)}, bf16[16,24,128]{2,1,0:T(8,128)(2,1)S(1)}, u32[]{:S(2)}, u32[]{:S(2)}) collective-permute-start(bf16[16,24,128]{2,1,0:T(8,128)(2,1)S(1)} %get-tuple-element.31.high), channel_id=1, source_target_pairs={{0,7},{1,2},{2,1},{3,4},{4,3},{5,6},{6,5},{7,0},{8,15},{9,10},{10,... | collective-permute-start | bytes 294920 | tf_op jit(solution)/shard_map/ppermute | solution.py:42
  29.5 5.6 %collective-permute-start.10 = (bf16[16,24,128]{2,1,0:T(8,128)(2,1)S(1)}, bf16[16,24,128]{2,1,0:T(8,128)(2,1)S(1)}, u32[]{:S(2)}, u32[]{:S(2)}) collective-permute-start(bf16[16,24,128]{2,1,0:T(8,128)(2,1)S(1)} %get-tuple-element.31.high), channel_id=1, source_target_pairs={{0,1},{1,0},{2,3},{3,2},{4,5},{5,4},{6,7},{7,6},{8,9},{9,8},{10,11... | collective-permute-start | bytes 294920 | tf_op jit(solution)/shard_map/ppermute | solution.py:42
  29.5 5.6 %collective-permute-start.9 = (bf16[16,24,128]{2,1,0:T(8,128)(2,1)S(1)}, bf16[16,24,128]{2,1,0:T(8,128)(2,1)S(1)}, u32[]{:S(2)}, u32[]{:S(2)}) collective-permute-start(bf16[16,24,128]{2,1,0:T(8,128)(2,1)S(1)} %get-tuple-element.31.high), channel_id=1, source_target_pairs={{0,24},{8,16},{16,8},{24,0},{1,25},{9,17},{17,9},{25,1},{2,26},{10... | collective-permute-start | bytes 294920 | tf_op jit(solution)/shard_map/ppermute | solution.py:42
  29.5 5.6 %collective-permute-start.8 = (bf16[16,24,128]{2,1,0:T(8,128)(2,1)S(1)}, bf16[16,24,128]{2,1,0:T(8,128)(2,1)S(1)}, u32[]{:S(2)}, u32[]{:S(2)}) collective-permute-start(bf16[16,24,128]{2,1,0:T(8,128)(2,1)S(1)} %get-tuple-element.31.high), channel_id=1, source_target_pairs={{0,8},{8,0},{16,24},{24,16},{1,9},{9,1},{17,25},{25,17},{2,10},{10... | collective-permute-start | bytes 294920 | tf_op jit(solution)/shard_map/ppermute | solution.py:42

commit v2 on v1

--- a/solution.py
+++ b/solution.py
@@ -8,8 +8,10 @@
 from jax.sharding import PartitionSpec as P
 
 ITERS = 3
+BASIS = 6
 SHIFT = 3.0
 EACH = 2
+WAVE = 2
 LIMIT = 16 * 1024 * 1024
 F32 = jnp.float32
 BF16 = jnp.bfloat16
@@ -36,11 +38,13 @@
 
 
 def exchange(high):
-    planes = {}
-    for axis in ("dev", "grp"):
-        first, second = pairings(lax.axis_size(axis))
-        planes[axis] = (lax.ppermute(high, axis, second), lax.ppermute(high, axis, first))
-    return planes["grp"][1], planes["grp"][0], planes["dev"][1], planes["dev"][0]
+    z_first, z_second = pairings(lax.axis_size("dev"))
+    t_first, t_second = pairings(lax.axis_size("grp"))
+    t_two = lax.ppermute(high, "grp", t_second)
+    z_two = lax.ppermute(high, "dev", z_second)
+    z_one = lax.ppermute(high, "dev", z_first)
+    t_one = lax.ppermute(high, "grp", t_first)
+    return t_one, t_two, z_one, z_two
 
 
 def lanes(shape):
@@ -190,21 +194,27 @@
         rest_ref[s] = joined(extra[0], rows)
 
 
-def later_local_kernel(dims, with_rest, high, low, *refs):
-    if with_rest:
-        rest, oper_ref, part_ref, rest_out, xy = refs
-    else:
-        oper_ref, part_ref, xy = refs
+def second_local_kernel(dims, high, low, rest, oper_ref, part_ref, rest_ref, xy):
     sites = xy.shape[0]
     rows = high.shape[1]
     for s in range(sites):
         xy[s] = stacked(high[s])
     for s in range(sites):
-        extra = [low[s]] + ([rest[s]] if with_rest else [])
-        total, more = local_product(s, dims, oper_ref[s], xy, extra)
+        total, more = local_product(s, dims, oper_ref[s], xy, [low[s], rest[s]])
         part_ref[s] = joined(total + more[0], rows)
-        if with_rest:
-            rest_out[s] = joined(more[1], rows)
+        rest_ref[s] = joined(more[1], rows)
+
+
+def third_local_kernel(dims, high, low, r0, v1, w1, v2, w2, oper_ref, part_ref, sums_ref, xy):
+    sites = xy.shape[0]
+    rows = high.shape[1]
+    for s in range(sites):
+        xy[s] = stacked(high[s])
+    for s in range(sites):
+        total, more = local_product(s, dims, oper_ref[s], xy, [low[s]])
+        part_ref[s] = joined(total + more[0], rows)
+    basis = [r0, v1, w1, v2, w2]
+    sums_ref[...] = inner_sums(basis, {k: i for k, i in slots(BASIS).items() if k[1] < BASIS - 1})
 
 
 def halo_value(s, flips, planes, part, before, oper_ref):
@@ -238,26 +248,32 @@
     return table
 
 
-def last_kernel(t_one, t_two, z_one, z_two, part, r0, v1, w1, v2, w2, oper_ref, v3, sums_ref):
-    flips = (swapped("grp"), swapped("dev"))
-    sites, rows, wide = part.shape
+def inner_sums(basis, table):
+    sites, rows, wide = basis[0].shape
     half = wide // 2
-    for s in range(sites):
-        v3[s] = halo_value(s, flips, ((t_one, t_two), (z_one, z_two)), part, v2, oper_ref)
-    basis = [r0, v1, w1, v2, w2, v3]
-    table = slots(len(basis))
     total = {key: jnp.zeros((rows, wide), F32) for key in table}
     for s in range(sites):
         plain = [b[s] for b in basis]
-        turned = [pltpu.roll(p, half, 1) for p in plain]
-        for i, j, part_of in table:
-            total[(i, j, part_of)] += plain[i] * (turned[j] if part_of else plain[j])
-    sign = jnp.where(lanes((rows, wide)) < half, 1.0, -1.0)
+        turned = {j: pltpu.roll(plain[j], half, 1) for j in sorted({k[1] for k in table if k[2]})}
+        for i, j, imaginary in table:
+            total[(i, j, imaginary)] += plain[i] * (turned[j] if imaginary else plain[j])
     lane = lanes((rows, wide))
+    sign = jnp.where(lane < half, 1.0, -1.0)
     packed = jnp.zeros((rows, wide), F32)
     for key, slot in table.items():
         value = total[key] * sign if key[2] else total[key]
         packed = jnp.where(lane == slot, jnp.sum(value, axis=1, keepdims=True), packed)
+    return packed
+
+
+def last_kernel(t_one, t_two, z_one, z_two, part, r0, v1, w1, v2, w2, early, oper_ref, v3, sums_ref):
+    flips = (swapped("grp"), swapped("dev"))
+    sites, rows, wide = part.shape
+    for s in range(sites):
+        v3[s] = halo_value(s, flips, ((t_one, t_two), (z_one, z_two)), part, v2, oper_ref)
+    table = slots(BASIS)
+    late = inner_sums([r0, v1, w1, v2, w2, v3], {k: i for k, i in table.items() if k[1] == BASIS - 1})
+    packed = early[...] + late
     square = jnp.concatenate([packed, jnp.zeros((wide - rows, wide), F32)], axis=0).T
     dense = jnp.zeros((8, wide), F32)
     for group in range(-(-len(table) // 8)):
@@ -309,7 +325,7 @@
             return (gram[(i, j, 0)], gram[(i, j, 1)])
         return (gram[(j, i, 0)], -gram[(j, i, 1)])
 
-    count = 6
+    count = BASIS
 
     def lower(a):
         out = []
@@ -374,7 +390,7 @@
     for d in range(1, sums.shape[0]):
         dense = dense + sums[d]
     basis = [r0, v1, w1, v2, w2, v3]
-    table = slots(len(basis))
+    table = slots(BASIS)
     turned = [dense if g == 0 else pltpu.roll(dense, wide - rows * g, 1) for g in range(-(-len(table) // 8))]
     gram = {key: turned[slot // 8][slot % 8 : slot % 8 + 1] for key, slot in table.items()}
     answer, residual = recurrences(gram, jnp.ones((1, wide), F32))
@@ -388,32 +404,36 @@
         coef[2 * e : 2 * e + 1] = value[0]
         coef[2 * e + 1 : 2 * e + 2] = value[1]
     columns = coef[...].T[:rows]
-    sign = jnp.where(lanes((rows, wide)) < half, -1.0, 1.0)
+    sign = jnp.where(lanes((8, wide)) < half, -1.0, 1.0)
     spread = [
         (
             which,
             index,
             jnp.broadcast_to(columns[:, 2 * e : 2 * e + 1], (rows, wide)),
-            jnp.broadcast_to(columns[:, 2 * e + 1 : 2 * e + 2], (rows, wide)) * sign,
+            jnp.broadcast_to(columns[:, 2 * e + 1 : 2 * e + 2], (rows, wide)),
         )
         for e, (which, index, _) in enumerate(entries)
     ]
-    lane = lanes((rows, wide))
-    def combined(s):
-        plain = [b[s] for b in basis]
-        rolled = [pltpu.roll(p, half, 1) for p in plain]
-        out = [jnp.zeros((rows, wide), F32), jnp.zeros((rows, wide), F32)]
-        for which, index, re, im in spread:
-            out[which] = out[which] + re * plain[index] + im * rolled[index]
-        resid[s] = out[1]
+    low = lanes((8, wide)) < quarter
+
+    def combined(s, block):
+        span = slice(8 * block, 8 * block + 8)
+        plain = [b[s, span, :] for b in basis]
+        out = []
+        for which in range(2):
+            terms = [(re[span] * plain[i], im[span] * plain[i]) for w, i, re, im in spread if w == which]
+            re, im = functools.reduce(plus, terms)
+            out.append(re + pltpu.roll(im, half, 1) * sign)
+        resid[s, span, :] = out[1]
         x = out[0].astype(BF16).astype(F32)
         by1 = pltpu.roll(x, wide - quarter, 1)
         by2 = pltpu.roll(x, half, 1)
         by3 = pltpu.roll(x, quarter, 1)
-        mixed[s, 0, pl.ds(0, rows, 2), :] = jnp.where(lane < quarter, x, -by1)
-        mixed[s, 0, pl.ds(1, rows, 2), :] = jnp.where(lane < quarter, by2, by3)
-        mixed[s, 1, pl.ds(0, rows, 2), :] = jnp.where(lane < quarter, by1, -by2)
-        mixed[s, 1, pl.ds(1, rows, 2), :] = jnp.where(lane < quarter, by3, x)
+        even, odd = pl.ds(16 * block, 8, 2), pl.ds(16 * block + 1, 8, 2)
+        mixed[s, 0, even, :] = jnp.where(low, x, -by1)
+        mixed[s, 0, odd, :] = jnp.where(low, by2, by3)
+        mixed[s, 1, even, :] = jnp.where(low, by1, -by2)
+        mixed[s, 1, odd, :] = jnp.where(low, by3, x)
 
     def prolonged(s):
         for h in range(2):
@@ -426,10 +446,11 @@
     groups = sem.shape[0]
     copies = []
     for g in range(groups + 1):
-        if g < groups:
-            for s in range(g * EACH, (g + 1) * EACH):
-                combined(s)
-        if g == groups - 1:
+        if g < groups and g % WAVE == 0:
+            for block in range(rows // 8):
+                for s in range(g * EACH, (g + WAVE) * EACH):
+                    combined(s, block)
+        if g == groups - WAVE:
             copies.append(pltpu.make_async_copy(resid, resid_hbm, resid_sem))
             copies[-1].start()
         if g:
@@ -500,7 +521,7 @@
 
     planes = exchange(h1)
     part, w2 = pl.pallas_call(
-        functools.partial(later_local_kernel, dims, True),
+        functools.partial(second_local_kernel, dims),
         in_specs=[VM] * 4,
         out_specs=[VM] * 2,
         out_shape=[vector, vector],
@@ -518,24 +539,24 @@
     )(*planes, part, v1, oper)
 
     planes = exchange(h2)
-    part = pl.pallas_call(
-        functools.partial(later_local_kernel, dims, False),
-        in_specs=[VM] * 3,
-        out_specs=VM,
-        out_shape=vector,
+    part, early = pl.pallas_call(
+        functools.partial(third_local_kernel, dims),
+        in_specs=[VM] * 8,
+        out_specs=[VM] * 2,
+        out_shape=[vector, jax.ShapeDtypeStruct((nrhs, wide), F32)],
         scratch_shapes=[xy],
         compiler_params=PARAMS,
         name="local_3",
-    )(h2, l2, oper)
+    )(h2, l2, r0, v1, w1, v2, w2, oper)
     devices = lax.axis_size("grp") * lax.axis_size("dev")
     v3, sums = pl.pallas_call(
         last_kernel,
-        in_specs=[VM] * 11,
+        in_specs=[VM] * 12,
         out_specs=[VM] * 2,
         out_shape=[vector, jax.ShapeDtypeStruct((devices, 8, wide), F32)],
         compiler_params=PARAMS,
         name="halo_3",
-    )(*planes, part, r0, v1, w1, v2, w2, oper)
+    )(*planes, part, r0, v1, w1, v2, w2, early, oper)
 
     sums = lax.all_to_all(sums, ("grp", "dev"), 0, 0)
     correction, residual = finish(sums, r0, v1, w1, v2, w2, v3, near)

time: 50.5 us -> 49.9 us (0.988)
  transfers between devices with their start and end apart: 12 -> 12, of which waited for: 7 -> 7; matrix products, arithmetic and copies ran while one was open for 0% -> 0% of each run, Pallas kernels for 4% -> 5%
where the time goes in v2:
time: 49.9 us; the launch traced here: 49.8 us
  starting transfers between devices  15.2 us (30%)
  Pallas kernels  12.7 us (25%)
  waiting for transfers between devices  10.6 us (21%)
  blocking collectives  10.6 us (21%)
  between operations  0.68 us (1%)
    ppermute x3, starting transfers between devices, exchange(): z_two = lax.ppermute(high, 'dev', z_second)  11.2 us
    all_to_all x1, blocking collectives, on_device(): sums = lax.all_to_all(sums, ('grp', 'dev'), 0, 0)  10.6 us
    ppermute x3, waiting for transfers between devices, exchange(): z_two = lax.ppermute(high, 'dev', z_second)  6.45 us
    pallas_call x1, Pallas kernels, restrict(): pl.pallas_call(restrict_kernel, in_specs=[HBM] * 3, out_specs=[VM] * 5, o...  5.07 us
    ppermute x3, waiting for transfers between devices, exchange(): z_one = lax.ppermute(high, 'dev', z_first)  3.99 us
    ppermute x3, starting transfers between devices, exchange(): t_one = lax.ppermute(high, 'grp', t_first)  3.34 us
    pallas_call x1, Pallas kernels, finish(): pl.pallas_call(finish_kernel, in_specs=[VM] * 8, out_specs=[HBM, HBM], ou...  3.27 us
    pallas_call x2, Pallas kernels, on_device(): pl.pallas_call(halo_kernel, in_specs=[VM] * 7, out_specs=[VM] * 3, out_sh...  1.11 us
  transfers between devices with their start and end apart: 12, of which 7 were waited for; matrix products, arithmetic and copies ran while one was open for 0% of the time, Pallas kernels for 5%

profile of v2, /device:TPU:0, one launch (start us, length us, event | category | flops | bytes accessed | tf_op | source)
XLA Modules:
  0.0 49.8 jit_solution(9776214374997084238)
XLA Ops:
  0.6 5.1 %restrict.1 = (f32[16,24,128]{2,1,0:T(8,128)S(1)}, bf16[16,24,128]{2,1,0:T(8,128)(2,1)S(1)}, bf16[16,24,128]{2,1,0:T(8,128)(2,1)S(1)}, bf16[16,64,3072]{2,1,0:T(8,128)(2,1)S(1)}, bf16[16,64,1152]{2,1,0:T(8,128)(2,1)S(1)}) custom-call(bf16[16,24,2,3072]{3,2,1,0:T(2,128)(2,1)} %bitcast.7, bf16[16,64,3072]{2,1,0:T(8,128)(2,1)} %bitcast.6, ...), custom_call_target="tpu_custom_call" | custom-call | tf_op jit(solution)/shard_map/restrict/pallas_call | solution.py:140
  5.7 6.1 %collective-permute-start.3 = (bf16[16,24,128]{2,1,0:T(8,128)(2,1)S(1)}, bf16[16,24,128]{2,1,0:T(8,128)(2,1)S(1)}, u32[]{:S(2)}, u32[]{:S(2)}) collective-permute-start(bf16[16,24,128]{2,1,0:T(8,128)(2,1)S(1)} %get-tuple-element.23.high), channel_id=1, source_target_pairs={{0,7},{1,2},{2,1},{3,4},{4,3},{5,6},{6,5},{7,0},{8,15},{9,10},{10,... | collective-permute-start | bytes 294920 | tf_op jit(solution)/shard_map/ppermute | solution.py:44
  11.8 0.0 collective-permute-start.2
  11.8 0.7 %collective-permute-start.1 = (bf16[16,24,128]{2,1,0:T(8,128)(2,1)S(1)}, bf16[16,24,128]{2,1,0:T(8,128)(2,1)S(1)}, u32[]{:S(2)}, u32[]{:S(2)}) collective-permute-start(bf16[16,24,128]{2,1,0:T(8,128)(2,1)S(1)} %get-tuple-element.23.high), channel_id=1, source_target_pairs={{0,24},{8,16},{16,8},{24,0},{1,25},{9,17},{17,9},{25,1},{2,26},{10... | collective-permute-start | bytes 294920 | tf_op jit(solution)/shard_map/ppermute | solution.py:43
  12.4 1.0 %collective-permute-start = (bf16[16,24,128]{2,1,0:T(8,128)(2,1)S(1)}, bf16[16,24,128]{2,1,0:T(8,128)(2,1)S(1)}, u32[]{:S(2)}, u32[]{:S(2)}) collective-permute-start(bf16[16,24,128]{2,1,0:T(8,128)(2,1)S(1)} %get-tuple-element.23.high), channel_id=1, source_target_pairs={{0,8},{8,0},{16,24},{24,16},{1,9},{9,1},{17,25},{25,17},{2,10},{10... | collective-permute-start | bytes 294920 | tf_op jit(solution)/shard_map/ppermute | solution.py:46
  13.4 0.7 %local_1.1 = (f32[16,24,128]{2,1,0:T(8,128)S(1)}, f32[16,24,128]{2,1,0:T(8,128)S(1)}) custom-call(bf16[16,24,128]{2,1,0:T(8,128)(2,1)S(1)} %get-tuple-element.23.high, bf16[16,24,128]{2,1,0:T(8,128)(2,1)S(1)} %get-tuple-element.24.low, bf16[16,64,1152]{2,1,0:T(8,128)(2,1)S(1)} %get-tuple-element.25.oper_ref), custom_call_target="tpu_custom_call" | custom-call | tf_op jit(solution)/shard_map/local_1/pallas_call | solution.py:504
  14.1 0.6 %collective-permute-done.3.z_two = bf16[16,24,128]{2,1,0:T(8,128)(2,1)S(1)} collective-permute-done((bf16[16,24,128]{2,1,0:T(8,128)(2,1)S(1)}, bf16[16,24,128]{2,1,0:T(8,128)(2,1)S(1)}, u32[]{:S(2)}, u32[]{:S(2)}) %collective-permute-start.3) | collective-permute-done | bytes 98336 | tf_op jit(solution)/shard_map/ppermute | solution.py:44
  14.6 2.0 %collective-permute-done.2.z_one = bf16[16,24,128]{2,1,0:T(8,128)(2,1)S(1)} collective-permute-done((bf16[16,24,128]{2,1,0:T(8,128)(2,1)S(1)}, bf16[16,24,128]{2,1,0:T(8,128)(2,1)S(1)}, u32[]{:S(2)}, u32[]{:S(2)}) %collective-permute-start.2) | collective-permute-done | bytes 98336 | tf_op jit(solution)/shard_map/ppermute | solution.py:45
  16.7 0.2 collective-permute-done.1.t_two
  16.8 0.6 %halo_1.1 = (f32[16,24,128]{2,1,0:T(8,128)S(1)}, bf16[16,24,128]{2,1,0:T(8,128)(2,1)S(1)}, bf16[16,24,128]{2,1,0:T(8,128)(2,1)S(1)}) custom-call(bf16[16,24,128]{2,1,0:T(8,128)(2,1)S(1)} %collective-permute-done.t_one, bf16[16,24,128]{2,1,0:T(8,128)(2,1)S(1)} %collective-permute-done.1.t_two, bf16[16,24,128]{2,1,0:T(8,128)(2,1)S(1)} %collective-permute-done.2.z_one, ...), custom_call_target="tpu_custom_call" | custom-call | tf_op jit(solution)/shard_map/halo_1/pallas_call | solution.py:513
  17.4 2.3 %collective-permute-start.7 = (bf16[16,24,128]{2,1,0:T(8,128)(2,1)S(1)}, bf16[16,24,128]{2,1,0:T(8,128)(2,1)S(1)}, u32[]{:S(2)}, u32[]{:S(2)}) collective-permute-start(bf16[16,24,128]{2,1,0:T(8,128)(2,1)S(1)} %get-tuple-element.28.high), channel_id=1, source_target_pairs={{0,7},{1,2},{2,1},{3,4},{4,3},{5,6},{6,5},{7,0},{8,15},{9,10},{10,... | collective-permute-start | bytes 294920 | tf_op jit(solution)/shard_map/ppermute | solution.py:44
  19.7 1.6 %collective-permute-start.4 = (bf16[16,24,128]{2,1,0:T(8,128)(2,1)S(1)}, bf16[16,24,128]{2,1,0:T(8,128)(2,1)S(1)}, u32[]{:S(2)}, u32[]{:S(2)}) collective-permute-start(bf16[16,24,128]{2,1,0:T(8,128)(2,1)S(1)} %get-tuple-element.28.high), channel_id=1, source_target_pairs={{0,8},{8,0},{16,24},{24,16},{1,9},{9,1},{17,25},{25,17},{2,10},{10... | collective-permute-start | bytes 294920 | tf_op jit(solution)/shard_map/ppermute | solution.py:46
  21.3 0.9 %local_2.1 = (f32[16,24,128]{2,1,0:T(8,128)S(1)}, f32[16,24,128]{2,1,0:T(8,128)S(1)}) custom-call(bf16[16,24,128]{2,1,0:T(8,128)(2,1)S(1)} %get-tuple-element.28.high, bf16[16,24,128]{2,1,0:T(8,128)(2,1)S(1)} %get-tuple-element.29.low, f32[16,24,128]{2,1,0:T(8,128)S(1)} %get-tuple-element.30.rest.w1, bf16[16,64,1152]{2,1,0:T(8,128)(2,1)S(1)} %get-tuple-element.25.oper_ref), custom_call_target="tpu_custom_call" | custom-call | tf_op jit(solution)/shard_map/local_2/pallas_call | solution.py:523
  22.2 2.9 %collective-permute-done.7.z_two = bf16[16,24,128]{2,1,0:T(8,128)(2,1)S(1)} collective-permute-done((bf16[16,24,128]{2,1,0:T(8,128)(2,1)S(1)}, bf16[16,24,128]{2,1,0:T(8,128)(2,1)S(1)}, u32[]{:S(2)}, u32[]{:S(2)}) %collective-permute-start.7) | collective-permute-done | bytes 98336 | tf_op jit(solution)/shard_map/ppermute | solution.py:44
  25.1 1.0 %collective-permute-done.6.z_one = bf16[16,24,128]{2,1,0:T(8,128)(2,1)S(1)} collective-permute-done((bf16[16,24,128]{2,1,0:T(8,128)(2,1)S(1)}, bf16[16,24,128]{2,1,0:T(8,128)(2,1)S(1)}, u32[]{:S(2)}, u32[]{:S(2)}) %collective-permute-start.6) | collective-permute-done | bytes 98336 | tf_op jit(solution)/shard_map/ppermute | solution.py:45
  26.1 0.6 %halo_2.1 = (f32[16,24,128]{2,1,0:T(8,128)S(1)}, bf16[16,24,128]{2,1,0:T(8,128)(2,1)S(1)}, bf16[16,24,128]{2,1,0:T(8,128)(2,1)S(1)}) custom-call(bf16[16,24,128]{2,1,0:T(8,128)(2,1)S(1)} %collective-permute-done.4.t_one, bf16[16,24,128]{2,1,0:T(8,128)(2,1)S(1)} %collective-permute-done.5.t_two, bf16[16,24,128]{2,1,0:T(8,128)(2,1)S(1)} %collective-permute-done.6.z_one, ...), custom_call_target="tpu_custom_call" | custom-call | tf_op jit(solution)/shard_map/halo_2/pallas_call | solution.py:532
  26.6 2.8 %collective-permute-start.11 = (bf16[16,24,128]{2,1,0:T(8,128)(2,1)S(1)}, bf16[16,24,128]{2,1,0:T(8,128)(2,1)S(1)}, u32[]{:S(2)}, u32[]{:S(2)}) collective-permute-start(bf16[16,24,128]{2,1,0:T(8,128)(2,1)S(1)} %get-tuple-element.33.high), channel_id=1, source_target_pairs={{0,7},{1,2},{2,1},{3,4},{4,3},{5,6},{6,5},{7,0},{8,15},{9,10},{10,... | collective-permute-start | bytes 294920 | tf_op jit(solution)/shard_map/ppermute | solution.py:44
  29.5 0.8 %collective-permute-start.8 = (bf16[16,24,128]{2,1,0:T(8,128)(2,1)S(1)}, bf16[16,24,128]{2,1,0:T(8,128)(2,1)S(1)}, u32[]{:S(2)}, u32[]{:S(2)}) collective-permute-start(bf16[16,24,128]{2,1,0:T(8,128)(2,1)S(1)} %get-tuple-element.33.high), channel_id=1, source_target_pairs={{0,8},{8,0},{16,24},{24,16},{1,9},{9,1},{17,25},{25,17},{2,10},{10... | collective-permute-start | bytes 294920 | tf_op jit(solution)/shard_map/ppermute | solution.py:46
  30.2 0.8 %local_3.1 = (f32[16,24,128]{2,1,0:T(8,128)S(1)}, f32[24,128]{1,0:T(8,128)S(1)}) custom-call(bf16[16,24,128]{2,1,0:T(8,128)(2,1)S(1)} %get-tuple-element.33.high, bf16[16,24,128]{2,1,0:T(8,128)(2,1)S(1)} %get-tuple-element.34.low, f32[16,24,128]{2,1,0:T(8,128)S(1)} %get-tuple-element.27.before.r0, f32[16,24,128]{2,1,0:T(8,128)S(1)} %get-tuple-element.32.before.v1, ...), custom_call_target="tpu_custom_call" | custom-call | tf_op jit(solution)/shard_map/local_3/pallas_call | solution.py:542
  31.1 3.0 %collective-permute-done.11.z_two = bf16[16,24,128]{2,1,0:T(8,128)(2,1)S(1)} collective-permute-done((bf16[16,24,128]{2,1,0:T(8,128)(2,1)S(1)}, bf16[16,24,128]{2,1,0:T(8,128)(2,1)S(1)}, u32[]{:S(2)}, u32[]{:S(2)}) %collective-permute-start.11) | collective-permute-done | bytes 98336 | tf_op jit(solution)/shard_map/ppermute | solution.py:44
  34.1 1.0 %collective-permute-done.10.z_one = bf16[16,24,128]{2,1,0:T(8,128)(2,1)S(1)} collective-permute-done((bf16[16,24,128]{2,1,0:T(8,128)(2,1)S(1)}, bf16[16,24,128]{2,1,0:T(8,128)(2,1)S(1)}, u32[]{:S(2)}, u32[]{:S(2)}) %collective-permute-start.10) | collective-permute-done | bytes 98336 | tf_op jit(solution)/shard_map/ppermute | solution.py:45
  35.1 0.9 %halo_3.1 = (f32[16,24,128]{2,1,0:T(8,128)S(1)}, f32[32,8,128]{2,1,0:T(8,128)S(1)}) custom-call(bf16[16,24,128]{2,1,0:T(8,128)(2,1)S(1)} %collective-permute-done.8.t_one, bf16[16,24,128]{2,1,0:T(8,128)(2,1)S(1)} %collective-permute-done.9.t_two, bf16[16,24,128]{2,1,0:T(8,128)(2,1)S(1)} %collective-permute-done.10.z_one, ...), custom_call_target="tpu_custom_call" | custom-call | tf_op jit(solution)/shard_map/halo_3/pallas_call | solution.py:552
  35.9 10.6 %all_to_all.5.sums = f32[32,8,128]{2,1,0:T(8,128)S(1)} all-to-all(f32[32,8,128]{2,1,0:T(8,128)S(1)} %get-tuple-element.39), channel_id=1, replica_groups=mesh['grp'=4,'dev'=8] {'grp','dev'}, dimensions={0} | all-to-all | bytes 262144 | tf_op jit(solution)/shard_map/all_to_all | solution.py:561
  46.5 3.3 %finish.1 = (bf16[16,24,2,3072]{3,2,1,0:T(2,128)(2,1)}, f32[16,24,128]{2,1,0:T(8,128)}) custom-call(f32[32,8,128]{2,1,0:T(8,128)S(1)} %all_to_all.5.sums, f32[16,24,128]{2,1,0:T(8,128)S(1)} %get-tuple-element.27.before.r0, f32[16,24,128]{2,1,0:T(8,128)S(1)} %get-tuple-element.32.before.v1, f32[16,24,128]{2,1,0:T(8,128)S(1)} %get-tuple-element.30.rest.w1, ...), custom_call_target="tpu_custom_call" | custom-call | tf_op jit(solution)/shard_map/finish/pallas_call | solution.py:469
  (9 shorter events, 0.0 us)
Async XLA Ops:
  5.7 8.9 %collective-permute-start.3 = (bf16[16,24,128]{2,1,0:T(8,128)(2,1)S(1)}, bf16[16,24,128]{2,1,0:T(8,128)(2,1)S(1)}, u32[]{:S(2)}, u32[]{:S(2)}) collective-permute-start(bf16[16,24,128]{2,1,0:T(8,128)(2,1)S(1)} %get-tuple-element.23.high), channel_id=1, source_target_pairs={{0,7},{1,2},{2,1},{3,4},{4,3},{5,6},{6,5},{7,0},{8,15},{9,10},{10,... | collective-permute-start | bytes 294920 | tf_op jit(solution)/shard_map/ppermute | solution.py:44
  11.8 4.9 %collective-permute-start.2 = (bf16[16,24,128]{2,1,0:T(8,128)(2,1)S(1)}, bf16[16,24,128]{2,1,0:T(8,128)(2,1)S(1)}, u32[]{:S(2)}, u32[]{:S(2)}) collective-permute-start(bf16[16,24,128]{2,1,0:T(8,128)(2,1)S(1)} %get-tuple-element.23.high), channel_id=1, source_target_pairs={{0,1},{1,0},{2,3},{3,2},{4,5},{5,4},{6,7},{7,6},{8,9},{9,8},{10,11... | collective-permute-start | bytes 294920 | tf_op jit(solution)/shard_map/ppermute | solution.py:45
  11.8 5.1 %collective-permute-start.1 = (bf16[16,24,128]{2,1,0:T(8,128)(2,1)S(1)}, bf16[16,24,128]{2,1,0:T(8,128)(2,1)S(1)}, u32[]{:S(2)}, u32[]{:S(2)}) collective-permute-start(bf16[16,24,128]{2,1,0:T(8,128)(2,1)S(1)} %get-tuple-element.23.high), channel_id=1, source_target_pairs={{0,24},{8,16},{16,8},{24,0},{1,25},{9,17},{17,9},{25,1},{2,26},{10... | collective-permute-start | bytes 294920 | tf_op jit(solution)/shard_map/ppermute | solution.py:43
  12.4 4.4 %collective-permute-start = (bf16[16,24,128]{2,1,0:T(8,128)(2,1)S(1)}, bf16[16,24,128]{2,1,0:T(8,128)(2,1)S(1)}, u32[]{:S(2)}, u32[]{:S(2)}) collective-permute-start(bf16[16,24,128]{2,1,0:T(8,128)(2,1)S(1)} %get-tuple-element.23.high), channel_id=1, source_target_pairs={{0,8},{8,0},{16,24},{24,16},{1,9},{9,1},{17,25},{25,17},{2,10},{10... | collective-permute-start | bytes 294920 | tf_op jit(solution)/shard_map/ppermute | solution.py:46
  17.4 7.7 %collective-permute-start.7 = (bf16[16,24,128]{2,1,0:T(8,128)(2,1)S(1)}, bf16[16,24,128]{2,1,0:T(8,128)(2,1)S(1)}, u32[]{:S(2)}, u32[]{:S(2)}) collective-permute-start(bf16[16,24,128]{2,1,0:T(8,128)(2,1)S(1)} %get-tuple-element.28.high), channel_id=1, source_target_pairs={{0,7},{1,2},{2,1},{3,4},{4,3},{5,6},{6,5},{7,0},{8,15},{9,10},{10,... | collective-permute-start | bytes 294920 | tf_op jit(solution)/shard_map/ppermute | solution.py:44
  19.7 6.3 %collective-permute-start.6 = (bf16[16,24,128]{2,1,0:T(8,128)(2,1)S(1)}, bf16[16,24,128]{2,1,0:T(8,128)(2,1)S(1)}, u32[]{:S(2)}, u32[]{:S(2)}) collective-permute-start(bf16[16,24,128]{2,1,0:T(8,128)(2,1)S(1)} %get-tuple-element.28.high), channel_id=1, source_target_pairs={{0,1},{1,0},{2,3},{3,2},{4,5},{5,4},{6,7},{7,6},{8,9},{9,8},{10,11... | collective-permute-start | bytes 294920 | tf_op jit(solution)/shard_map/ppermute | solution.py:45
  19.7 6.3 %collective-permute-start.5 = (bf16[16,24,128]{2,1,0:T(8,128)(2,1)S(1)}, bf16[16,24,128]{2,1,0:T(8,128)(2,1)S(1)}, u32[]{:S(2)}, u32[]{:S(2)}) collective-permute-start(bf16[16,24,128]{2,1,0:T(8,128)(2,1)S(1)} %get-tuple-element.28.high), channel_id=1, source_target_pairs={{0,24},{8,16},{16,8},{24,0},{1,25},{9,17},{17,9},{25,1},{2,26},{10... | collective-permute-start | bytes 294920 | tf_op jit(solution)/shard_map/ppermute | solution.py:43
  19.7 6.3 %collective-permute-start.4 = (bf16[16,24,128]{2,1,0:T(8,128)(2,1)S(1)}, bf16[16,24,128]{2,1,0:T(8,128)(2,1)S(1)}, u32[]{:S(2)}, u32[]{:S(2)}) collective-permute-start(bf16[16,24,128]{2,1,0:T(8,128)(2,1)S(1)} %get-tuple-element.28.high), channel_id=1, source_target_pairs={{0,8},{8,0},{16,24},{24,16},{1,9},{9,1},{17,25},{25,17},{2,10},{10... | collective-permute-start | bytes 294920 | tf_op jit(solution)/shard_map/ppermute | solution.py:46
  26.6 7.5 %collective-permute-start.11 = (bf16[16,24,128]{2,1,0:T(8,128)(2,1)S(1)}, bf16[16,24,128]{2,1,0:T(8,128)(2,1)S(1)}, u32[]{:S(2)}, u32[]{:S(2)}) collective-permute-start(bf16[16,24,128]{2,1,0:T(8,128)(2,1)S(1)} %get-tuple-element.33.high), channel_id=1, source_target_pairs={{0,7},{1,2},{2,1},{3,4},{4,3},{5,6},{6,5},{7,0},{8,15},{9,10},{10,... | collective-permute-start | bytes 294920 | tf_op jit(solution)/shard_map/ppermute | solution.py:44
  29.5 5.6 %collective-permute-start.10 = (bf16[16,24,128]{2,1,0:T(8,128)(2,1)S(1)}, bf16[16,24,128]{2,1,0:T(8,128)(2,1)S(1)}, u32[]{:S(2)}, u32[]{:S(2)}) collective-permute-start(bf16[16,24,128]{2,1,0:T(8,128)(2,1)S(1)} %get-tuple-element.33.high), channel_id=1, source_target_pairs={{0,1},{1,0},{2,3},{3,2},{4,5},{5,4},{6,7},{7,6},{8,9},{9,8},{10,11... | collective-permute-start | bytes 294920 | tf_op jit(solution)/shard_map/ppermute | solution.py:45
  29.5 5.6 %collective-permute-start.9 = (bf16[16,24,128]{2,1,0:T(8,128)(2,1)S(1)}, bf16[16,24,128]{2,1,0:T(8,128)(2,1)S(1)}, u32[]{:S(2)}, u32[]{:S(2)}) collective-permute-start(bf16[16,24,128]{2,1,0:T(8,128)(2,1)S(1)} %get-tuple-element.33.high), channel_id=1, source_target_pairs={{0,24},{8,16},{16,8},{24,0},{1,25},{9,17},{17,9},{25,1},{2,26},{10... | collective-permute-start | bytes 294920 | tf_op jit(solution)/shard_map/ppermute | solution.py:43
  29.5 5.6 %collective-permute-start.8 = (bf16[16,24,128]{2,1,0:T(8,128)(2,1)S(1)}, bf16[16,24,128]{2,1,0:T(8,128)(2,1)S(1)}, u32[]{:S(2)}, u32[]{:S(2)}) collective-permute-start(bf16[16,24,128]{2,1,0:T(8,128)(2,1)S(1)} %get-tuple-element.33.high), channel_id=1, source_target_pairs={{0,8},{8,0},{16,24},{24,16},{1,9},{9,1},{17,25},{25,17},{2,10},{10... | collective-permute-start | bytes 294920 | tf_op jit(solution)/shard_map/ppermute | solution.py:46

commit v3 on v2

--- a/solution.py
+++ b/solution.py
@@ -68,18 +68,21 @@
     return jnp.concatenate([product[:rows], product[rows:]], axis=1)
 
 
+def batches(sites):
+    return [(s, EACH) for s in range(0, sites, EACH)]
+
+
 def restrict_kernel(
-    field_hbm, near_hbm, oper_hbm, source_ref, high_ref, low_ref, near_ref, oper_ref, field, prods, sem, oper_sem
+    field_hbm, near_hbm, source_ref, high_ref, low_ref, near_ref, field, prods, sem
 ):
     sites, nrhs = field.shape[:2]
     middle = field.shape[-1] // 2
     nvec = near_ref.shape[1] // 2
     wide = 4 * nvec
-    groups = sem.shape[1]
-    each = EACH
+    groups = batches(sites)
     copies = []
-    for g in range(groups):
-        span = pl.ds(g * each, each)
+    for g, (first, count) in enumerate(groups):
+        span = pl.ds(first, count)
         pair = (
             pltpu.make_async_copy(field_hbm.at[span], field.at[span], sem.at[0, g]),
             pltpu.make_async_copy(near_hbm.at[span], near_ref.at[span], sem.at[1, g]),
@@ -87,8 +90,6 @@
         for copy in pair:
             copy.start()
         copies.append(pair)
-    last = pltpu.make_async_copy(oper_hbm.at[lax.axis_index("grp")], oper_ref, oper_sem)
-    last.start()
     lane = lanes((nrhs, wide))
 
     def multiply(s):
@@ -122,41 +123,38 @@
         source_ref[s] = value
         high_ref[s], low_ref[s] = halves(value)
 
-    for g in range(groups + 1):
-        if g < groups:
+    for g in range(len(groups) + 1):
+        if g < len(groups):
             for copy in copies[g]:
                 copy.wait()
-            for s in range(g * each, (g + 1) * each):
+            for s in range(groups[g][0], sum(groups[g])):
                 multiply(s)
         if g:
-            for s in range((g - 1) * each, g * each):
+            for s in range(groups[g - 1][0], sum(groups[g - 1])):
                 arrange(s)
-    last.wait()
-
-
-def restrict(field, near, oper):
+
+
+def restrict(field, near):
     sites, nrhs, _, fine = field.shape
     coarse = 2 * near.shape[1]
     return pl.pallas_call(
         restrict_kernel,
-        in_specs=[HBM] * 3,
-        out_specs=[VM] * 5,
+        in_specs=[HBM] * 2,
+        out_specs=[VM] * 4,
         out_shape=[
             jax.ShapeDtypeStruct((sites, nrhs, coarse), F32),
             jax.ShapeDtypeStruct((sites, nrhs, coarse), BF16),
             jax.ShapeDtypeStruct((sites, nrhs, coarse), BF16),
             jax.ShapeDtypeStruct(near.shape, BF16),
-            jax.ShapeDtypeStruct(oper.shape[1:], BF16),
         ],
         scratch_shapes=[
             pltpu.VMEM(field.shape, BF16),
             pltpu.VMEM((sites, 2 * nrhs, coarse), F32),
-            pltpu.SemaphoreType.DMA((2, sites // EACH)),
-            pltpu.SemaphoreType.DMA,
+            pltpu.SemaphoreType.DMA((2, len(batches(sites)))),
         ],
         compiler_params=PARAMS,
         name="restrict",
-    )(field, near, oper)
+    )(field, near)
 
 
 def neighbours(s, ly, lx):
@@ -183,11 +181,14 @@
     return total, [centre[(i + 1) * rows : (i + 2) * rows] for i in range(len(extra))]
 
 
-def first_local_kernel(dims, high, low, oper_ref, part_ref, rest_ref, xy):
+def first_local_kernel(dims, high, low, oper_hbm, part_ref, rest_ref, oper_ref, xy, sem):
+    copy = pltpu.make_async_copy(oper_hbm.at[lax.axis_index("grp")], oper_ref, sem)
+    copy.start()
     sites = xy.shape[0]
     rows = high.shape[1]
     for s in range(sites):
         xy[s] = stacked(high[s])
+    copy.wait()
     for s in range(sites):
         total, extra = local_product(s, dims, oper_ref[s], xy, [low[s]])
         part_ref[s] = joined(total, rows)
@@ -274,11 +275,10 @@
     table = slots(BASIS)
     late = inner_sums([r0, v1, w1, v2, w2, v3], {k: i for k, i in table.items() if k[1] == BASIS - 1})
     packed = early[...] + late
-    square = jnp.concatenate([packed, jnp.zeros((wide - rows, wide), F32)], axis=0).T
-    dense = jnp.zeros((8, wide), F32)
-    for group in range(-(-len(table) // 8)):
-        piece = square[8 * group : 8 * group + 8]
-        dense = dense + (pltpu.roll(piece, rows * group, 1) if group else piece)
+    square = packed.T
+    groups = -(-len(table) // 8)
+    pieces = [square[8 * group : 8 * group + 8] for group in range(groups)]
+    dense = jnp.concatenate(pieces + [jnp.zeros((8, wide - rows * groups), F32)], axis=1)
     for d in range(sums_ref.shape[0]):
         sums_ref[d] = dense
 
@@ -498,15 +498,15 @@
     rounded = jax.ShapeDtypeStruct((sites, nrhs, wide), BF16)
     xy = pltpu.VMEM((sites, 2 * nrhs, wide), BF16)
 
-    r0, h0, l0, near, oper = restrict(field, near, oper)
+    r0, h0, l0, near = restrict(field, near)
 
     planes = exchange(h0)
-    part, w1 = pl.pallas_call(
+    part, w1, oper = pl.pallas_call(
         functools.partial(first_local_kernel, dims),
-        in_specs=[VM] * 3,
-        out_specs=[VM] * 2,
-        out_shape=[vector, vector],
-        scratch_shapes=[xy],
+        in_specs=[VM, VM, HBM],
+        out_specs=[VM] * 3,
+        out_shape=[vector, vector, jax.ShapeDtypeStruct(oper.shape[1:], BF16)],
+        scratch_shapes=[xy, pltpu.SemaphoreType.DMA],
         compiler_params=PARAMS,
         name="local_1",
     )(h0, l0, oper)

time: 49.9 us -> 49.9 us (level)
  waiting for transfers between devices: 10.6 us -> 8.85 us
  Pallas kernels: 12.7 us -> 14.4 us
    pallas_call x2, Pallas kernels: 5.76 us -> 7.35 us  [the longest x1 4.98 us: restrict(): pl.pallas_call(restrict_kernel, in_specs=[HBM] * 2, out_specs=[VM] * 4, o...]
    ppermute x3, waiting for transfers between devices: 3.99 us -> 2.84 us  [exchange(): z_one = lax.ppermute(high, 'dev', z_first)]
    ppermute x3, waiting for transfers between devices: 6.45 us -> 5.84 us  [exchange(): z_two = lax.ppermute(high, 'dev', z_second)]
  transfers between devices with their start and end apart: 12 -> 12, of which waited for: 7 -> 6; matrix products, arithmetic and copies ran while one was open for 0% -> 0% of each run, Pallas kernels for 5% -> 8%
where the time goes in v3:
time: 49.9 us; the launch traced here: 49.7 us
  starting transfers between devices  15.2 us (30%)
  Pallas kernels  14.4 us (29%)
  blocking collectives  10.6 us (21%)
  waiting for transfers between devices  8.85 us (18%)
  between operations  0.69 us (1%)
    ppermute x3, starting transfers between devices, exchange(): z_two = lax.ppermute(high, 'dev', z_second)  11.2 us
    all_to_all x1, blocking collectives, on_device(): sums = lax.all_to_all(sums, ('grp', 'dev'), 0, 0)  10.6 us
    ppermute x3, waiting for transfers between devices, exchange(): z_two = lax.ppermute(high, 'dev', z_second)  5.84 us
    pallas_call x1, Pallas kernels, restrict(): pl.pallas_call(restrict_kernel, in_specs=[HBM] * 2, out_specs=[VM] * 4, o...  4.98 us
    ppermute x3, starting transfers between devices, exchange(): t_one = lax.ppermute(high, 'grp', t_first)  3.34 us
    pallas_call x1, Pallas kernels, finish(): pl.pallas_call(finish_kernel, in_specs=[VM] * 8, out_specs=[HBM, HBM], ou...  3.25 us
    ppermute x3, waiting for transfers between devices, exchange(): z_one = lax.ppermute(high, 'dev', z_first)  2.84 us
    pallas_call x1, Pallas kernels, on_device(): pl.pallas_call(functools.partial(first_local_kernel, dims), in_specs=[VM,...  2.37 us
  transfers between devices with their start and end apart: 12, of which 6 were waited for; matrix products, arithmetic and copies ran while one was open for 0% of the time, Pallas kernels for 8%

profile of v3, /device:TPU:0, one launch (start us, length us, event | category | flops | bytes accessed | tf_op | source)
XLA Modules:
  0.0 49.7 jit_solution(11252568815730051557)
XLA Ops:
  0.6 5.0 %restrict.1 = (f32[16,24,128]{2,1,0:T(8,128)S(1)}, bf16[16,24,128]{2,1,0:T(8,128)(2,1)S(1)}, bf16[16,24,128]{2,1,0:T(8,128)(2,1)S(1)}, bf16[16,64,3072]{2,1,0:T(8,128)(2,1)S(1)}) custom-call(bf16[16,24,2,3072]{3,2,1,0:T(2,128)(2,1)} %bitcast.7, bf16[16,64,3072]{2,1,0:T(8,128)(2,1)} %bitcast.6), custom_call_target="tpu_custom_call" | custom-call | tf_op jit(solution)/shard_map/restrict/pallas_call | solution.py:140
  5.6 6.1 %collective-permute-start.3 = (bf16[16,24,128]{2,1,0:T(8,128)(2,1)S(1)}, bf16[16,24,128]{2,1,0:T(8,128)(2,1)S(1)}, u32[]{:S(2)}, u32[]{:S(2)}) collective-permute-start(bf16[16,24,128]{2,1,0:T(8,128)(2,1)S(1)} %get-tuple-element.23.high), channel_id=1, source_target_pairs={{0,7},{1,2},{2,1},{3,4},{4,3},{5,6},{6,5},{7,0},{8,15},{9,10},{10,... | collective-permute-start | bytes 294920 | tf_op jit(solution)/shard_map/ppermute | solution.py:44
  11.7 0.7 %collective-permute-start.1 = (bf16[16,24,128]{2,1,0:T(8,128)(2,1)S(1)}, bf16[16,24,128]{2,1,0:T(8,128)(2,1)S(1)}, u32[]{:S(2)}, u32[]{:S(2)}) collective-permute-start(bf16[16,24,128]{2,1,0:T(8,128)(2,1)S(1)} %get-tuple-element.23.high), channel_id=1, source_target_pairs={{0,24},{8,16},{16,8},{24,0},{1,25},{9,17},{17,9},{25,1},{2,26},{10... | collective-permute-start | bytes 294920 | tf_op jit(solution)/shard_map/ppermute | solution.py:43
  12.3 1.0 %collective-permute-start = (bf16[16,24,128]{2,1,0:T(8,128)(2,1)S(1)}, bf16[16,24,128]{2,1,0:T(8,128)(2,1)S(1)}, u32[]{:S(2)}, u32[]{:S(2)}) collective-permute-start(bf16[16,24,128]{2,1,0:T(8,128)(2,1)S(1)} %get-tuple-element.23.high), channel_id=1, source_target_pairs={{0,8},{8,0},{16,24},{24,16},{1,9},{9,1},{17,25},{25,17},{2,10},{10... | collective-permute-start | bytes 294920 | tf_op jit(solution)/shard_map/ppermute | solution.py:46
  13.3 2.4 %local_1.1 = (f32[16,24,128]{2,1,0:T(8,128)S(1)}, f32[16,24,128]{2,1,0:T(8,128)S(1)}, bf16[16,64,1152]{2,1,0:T(8,128)(2,1)S(1)}) custom-call(bf16[16,24,128]{2,1,0:T(8,128)(2,1)S(1)} %get-tuple-element.23.high, bf16[16,24,128]{2,1,0:T(8,128)(2,1)S(1)} %get-tuple-element.24.low, bf16[4,16,64,1152]{3,2,1,0:T(8,128)(2,1)} %bitcast.5), custom_call_target="tpu_custom_call" | custom-call | tf_op jit(solution)/shard_map/local_1/pallas_call | solution.py:504
  15.7 0.0 collective-permute-done.3.z_two
  15.7 0.9 %collective-permute-done.2.z_one = bf16[16,24,128]{2,1,0:T(8,128)(2,1)S(1)} collective-permute-done((bf16[16,24,128]{2,1,0:T(8,128)(2,1)S(1)}, bf16[16,24,128]{2,1,0:T(8,128)(2,1)S(1)}, u32[]{:S(2)}, u32[]{:S(2)}) %collective-permute-start.2) | collective-permute-done | bytes 98336 | tf_op jit(solution)/shard_map/ppermute | solution.py:45
  16.6 0.2 collective-permute-done.1.t_two
  16.7 0.0 collective-permute-done.t_one
  16.7 0.6 %halo_1.1 = (f32[16,24,128]{2,1,0:T(8,128)S(1)}, bf16[16,24,128]{2,1,0:T(8,128)(2,1)S(1)}, bf16[16,24,128]{2,1,0:T(8,128)(2,1)S(1)}) custom-call(bf16[16,24,128]{2,1,0:T(8,128)(2,1)S(1)} %collective-permute-done.t_one, bf16[16,24,128]{2,1,0:T(8,128)(2,1)S(1)} %collective-permute-done.1.t_two, bf16[16,24,128]{2,1,0:T(8,128)(2,1)S(1)} %collective-permute-done.2.z_one, ...), custom_call_target="tpu_custom_call" | custom-call | tf_op jit(solution)/shard_map/halo_1/pallas_call | solution.py:513
  17.3 2.3 %collective-permute-start.7 = (bf16[16,24,128]{2,1,0:T(8,128)(2,1)S(1)}, bf16[16,24,128]{2,1,0:T(8,128)(2,1)S(1)}, u32[]{:S(2)}, u32[]{:S(2)}) collective-permute-start(bf16[16,24,128]{2,1,0:T(8,128)(2,1)S(1)} %get-tuple-element.28.high), channel_id=1, source_target_pairs={{0,7},{1,2},{2,1},{3,4},{4,3},{5,6},{6,5},{7,0},{8,15},{9,10},{10,... | collective-permute-start | bytes 294920 | tf_op jit(solution)/shard_map/ppermute | solution.py:44
  19.7 1.6 %collective-permute-start.4 = (bf16[16,24,128]{2,1,0:T(8,128)(2,1)S(1)}, bf16[16,24,128]{2,1,0:T(8,128)(2,1)S(1)}, u32[]{:S(2)}, u32[]{:S(2)}) collective-permute-start(bf16[16,24,128]{2,1,0:T(8,128)(2,1)S(1)} %get-tuple-element.28.high), channel_id=1, source_target_pairs={{0,8},{8,0},{16,24},{24,16},{1,9},{9,1},{17,25},{25,17},{2,10},{10... | collective-permute-start | bytes 294920 | tf_op jit(solution)/shard_map/ppermute | solution.py:46
  21.3 0.9 %local_2.1 = (f32[16,24,128]{2,1,0:T(8,128)S(1)}, f32[16,24,128]{2,1,0:T(8,128)S(1)}) custom-call(bf16[16,24,128]{2,1,0:T(8,128)(2,1)S(1)} %get-tuple-element.28.high, bf16[16,24,128]{2,1,0:T(8,128)(2,1)S(1)} %get-tuple-element.29.low, f32[16,24,128]{2,1,0:T(8,128)S(1)} %get-tuple-element.30.rest.w1, bf16[16,64,1152]{2,1,0:T(8,128)(2,1)S(1)} %get-tuple-element.27.oper_ref), custom_call_target="tpu_custom_call" | custom-call | tf_op jit(solution)/shard_map/local_2/pallas_call | solution.py:523
  22.1 2.9 %collective-permute-done.7.z_two = bf16[16,24,128]{2,1,0:T(8,128)(2,1)S(1)} collective-permute-done((bf16[16,24,128]{2,1,0:T(8,128)(2,1)S(1)}, bf16[16,24,128]{2,1,0:T(8,128)(2,1)S(1)}, u32[]{:S(2)}, u32[]{:S(2)}) %collective-permute-start.7) | collective-permute-done | bytes 98336 | tf_op jit(solution)/shard_map/ppermute | solution.py:44
  25.0 1.0 %collective-permute-done.6.z_one = bf16[16,24,128]{2,1,0:T(8,128)(2,1)S(1)} collective-permute-done((bf16[16,24,128]{2,1,0:T(8,128)(2,1)S(1)}, bf16[16,24,128]{2,1,0:T(8,128)(2,1)S(1)}, u32[]{:S(2)}, u32[]{:S(2)}) %collective-permute-start.6) | collective-permute-done | bytes 98336 | tf_op jit(solution)/shard_map/ppermute | solution.py:45
  26.0 0.6 %halo_2.1 = (f32[16,24,128]{2,1,0:T(8,128)S(1)}, bf16[16,24,128]{2,1,0:T(8,128)(2,1)S(1)}, bf16[16,24,128]{2,1,0:T(8,128)(2,1)S(1)}) custom-call(bf16[16,24,128]{2,1,0:T(8,128)(2,1)S(1)} %collective-permute-done.4.t_one, bf16[16,24,128]{2,1,0:T(8,128)(2,1)S(1)} %collective-permute-done.5.t_two, bf16[16,24,128]{2,1,0:T(8,128)(2,1)S(1)} %collective-permute-done.6.z_one, ...), custom_call_target="tpu_custom_call" | custom-call | tf_op jit(solution)/shard_map/halo_2/pallas_call | solution.py:532
  26.6 2.8 %collective-permute-start.11 = (bf16[16,24,128]{2,1,0:T(8,128)(2,1)S(1)}, bf16[16,24,128]{2,1,0:T(8,128)(2,1)S(1)}, u32[]{:S(2)}, u32[]{:S(2)}) collective-permute-start(bf16[16,24,128]{2,1,0:T(8,128)(2,1)S(1)} %get-tuple-element.33.high), channel_id=1, source_target_pairs={{0,7},{1,2},{2,1},{3,4},{4,3},{5,6},{6,5},{7,0},{8,15},{9,10},{10,... | collective-permute-start | bytes 294920 | tf_op jit(solution)/shard_map/ppermute | solution.py:44
  29.4 0.8 %collective-permute-start.8 = (bf16[16,24,128]{2,1,0:T(8,128)(2,1)S(1)}, bf16[16,24,128]{2,1,0:T(8,128)(2,1)S(1)}, u32[]{:S(2)}, u32[]{:S(2)}) collective-permute-start(bf16[16,24,128]{2,1,0:T(8,128)(2,1)S(1)} %get-tuple-element.33.high), channel_id=1, source_target_pairs={{0,8},{8,0},{16,24},{24,16},{1,9},{9,1},{17,25},{25,17},{2,10},{10... | collective-permute-start | bytes 294920 | tf_op jit(solution)/shard_map/ppermute | solution.py:46
  30.2 0.9 %local_3.1 = (f32[16,24,128]{2,1,0:T(8,128)S(1)}, f32[24,128]{1,0:T(8,128)S(1)}) custom-call(bf16[16,24,128]{2,1,0:T(8,128)(2,1)S(1)} %get-tuple-element.33.high, bf16[16,24,128]{2,1,0:T(8,128)(2,1)S(1)} %get-tuple-element.34.low, f32[16,24,128]{2,1,0:T(8,128)S(1)} %get-tuple-element.26.before.r0, f32[16,24,128]{2,1,0:T(8,128)S(1)} %get-tuple-element.32.before.v1, ...), custom_call_target="tpu_custom_call" | custom-call | tf_op jit(solution)/shard_map/local_3/pallas_call | solution.py:542
  31.1 3.0 %collective-permute-done.11.z_two = bf16[16,24,128]{2,1,0:T(8,128)(2,1)S(1)} collective-permute-done((bf16[16,24,128]{2,1,0:T(8,128)(2,1)S(1)}, bf16[16,24,128]{2,1,0:T(8,128)(2,1)S(1)}, u32[]{:S(2)}, u32[]{:S(2)}) %collective-permute-start.11) | collective-permute-done | bytes 98336 | tf_op jit(solution)/shard_map/ppermute | solution.py:44
  34.1 1.0 %collective-permute-done.10.z_one = bf16[16,24,128]{2,1,0:T(8,128)(2,1)S(1)} collective-permute-done((bf16[16,24,128]{2,1,0:T(8,128)(2,1)S(1)}, bf16[16,24,128]{2,1,0:T(8,128)(2,1)S(1)}, u32[]{:S(2)}, u32[]{:S(2)}) %collective-permute-start.10) | collective-permute-done | bytes 98336 | tf_op jit(solution)/shard_map/ppermute | solution.py:45
  35.0 0.9 %halo_3.1 = (f32[16,24,128]{2,1,0:T(8,128)S(1)}, f32[32,8,128]{2,1,0:T(8,128)S(1)}) custom-call(bf16[16,24,128]{2,1,0:T(8,128)(2,1)S(1)} %collective-permute-done.8.t_one, bf16[16,24,128]{2,1,0:T(8,128)(2,1)S(1)} %collective-permute-done.9.t_two, bf16[16,24,128]{2,1,0:T(8,128)(2,1)S(1)} %collective-permute-done.10.z_one, ...), custom_call_target="tpu_custom_call" | custom-call | tf_op jit(solution)/shard_map/halo_3/pallas_call | solution.py:552
  35.9 10.6 %all_to_all.5.sums = f32[32,8,128]{2,1,0:T(8,128)S(1)} all-to-all(f32[32,8,128]{2,1,0:T(8,128)S(1)} %get-tuple-element.39), channel_id=1, replica_groups=mesh['grp'=4,'dev'=8] {'grp','dev'}, dimensions={0} | all-to-all | bytes 262144 | tf_op jit(solution)/shard_map/all_to_all | solution.py:561
  46.5 3.2 %finish.1 = (bf16[16,24,2,3072]{3,2,1,0:T(2,128)(2,1)}, f32[16,24,128]{2,1,0:T(8,128)}) custom-call(f32[32,8,128]{2,1,0:T(8,128)S(1)} %all_to_all.5.sums, f32[16,24,128]{2,1,0:T(8,128)S(1)} %get-tuple-element.26.before.r0, f32[16,24,128]{2,1,0:T(8,128)S(1)} %get-tuple-element.32.before.v1, f32[16,24,128]{2,1,0:T(8,128)S(1)} %get-tuple-element.30.rest.w1, ...), custom_call_target="tpu_custom_call" | custom-call | tf_op jit(solution)/shard_map/finish/pallas_call | solution.py:469
  (9 shorter events, 0.0 us)
Async XLA Ops:
  5.6 10.1 %collective-permute-start.3 = (bf16[16,24,128]{2,1,0:T(8,128)(2,1)S(1)}, bf16[16,24,128]{2,1,0:T(8,128)(2,1)S(1)}, u32[]{:S(2)}, u32[]{:S(2)}) collective-permute-start(bf16[16,24,128]{2,1,0:T(8,128)(2,1)S(1)} %get-tuple-element.23.high), channel_id=1, source_target_pairs={{0,7},{1,2},{2,1},{3,4},{4,3},{5,6},{6,5},{7,0},{8,15},{9,10},{10,... | collective-permute-start | bytes 294920 | tf_op jit(solution)/shard_map/ppermute | solution.py:44
  11.7 4.9 %collective-permute-start.2 = (bf16[16,24,128]{2,1,0:T(8,128)(2,1)S(1)}, bf16[16,24,128]{2,1,0:T(8,128)(2,1)S(1)}, u32[]{:S(2)}, u32[]{:S(2)}) collective-permute-start(bf16[16,24,128]{2,1,0:T(8,128)(2,1)S(1)} %get-tuple-element.23.high), channel_id=1, source_target_pairs={{0,1},{1,0},{2,3},{3,2},{4,5},{5,4},{6,7},{7,6},{8,9},{9,8},{10,11... | collective-permute-start | bytes 294920 | tf_op jit(solution)/shard_map/ppermute | solution.py:45
  11.7 5.1 %collective-permute-start.1 = (bf16[16,24,128]{2,1,0:T(8,128)(2,1)S(1)}, bf16[16,24,128]{2,1,0:T(8,128)(2,1)S(1)}, u32[]{:S(2)}, u32[]{:S(2)}) collective-permute-start(bf16[16,24,128]{2,1,0:T(8,128)(2,1)S(1)} %get-tuple-element.23.high), channel_id=1, source_target_pairs={{0,24},{8,16},{16,8},{24,0},{1,25},{9,17},{17,9},{25,1},{2,26},{10... | collective-permute-start | bytes 294920 | tf_op jit(solution)/shard_map/ppermute | solution.py:43
  12.3 4.4 %collective-permute-start = (bf16[16,24,128]{2,1,0:T(8,128)(2,1)S(1)}, bf16[16,24,128]{2,1,0:T(8,128)(2,1)S(1)}, u32[]{:S(2)}, u32[]{:S(2)}) collective-permute-start(bf16[16,24,128]{2,1,0:T(8,128)(2,1)S(1)} %get-tuple-element.23.high), channel_id=1, source_target_pairs={{0,8},{8,0},{16,24},{24,16},{1,9},{9,1},{17,25},{25,17},{2,10},{10... | collective-permute-start | bytes 294920 | tf_op jit(solution)/shard_map/ppermute | solution.py:46
  17.3 7.7 %collective-permute-start.7 = (bf16[16,24,128]{2,1,0:T(8,128)(2,1)S(1)}, bf16[16,24,128]{2,1,0:T(8,128)(2,1)S(1)}, u32[]{:S(2)}, u32[]{:S(2)}) collective-permute-start(bf16[16,24,128]{2,1,0:T(8,128)(2,1)S(1)} %get-tuple-element.28.high), channel_id=1, source_target_pairs={{0,7},{1,2},{2,1},{3,4},{4,3},{5,6},{6,5},{7,0},{8,15},{9,10},{10,... | collective-permute-start | bytes 294920 | tf_op jit(solution)/shard_map/ppermute | solution.py:44
  19.7 6.3 %collective-permute-start.6 = (bf16[16,24,128]{2,1,0:T(8,128)(2,1)S(1)}, bf16[16,24,128]{2,1,0:T(8,128)(2,1)S(1)}, u32[]{:S(2)}, u32[]{:S(2)}) collective-permute-start(bf16[16,24,128]{2,1,0:T(8,128)(2,1)S(1)} %get-tuple-element.28.high), channel_id=1, source_target_pairs={{0,1},{1,0},{2,3},{3,2},{4,5},{5,4},{6,7},{7,6},{8,9},{9,8},{10,11... | collective-permute-start | bytes 294920 | tf_op jit(solution)/shard_map/ppermute | solution.py:45
  19.7 6.3 %collective-permute-start.5 = (bf16[16,24,128]{2,1,0:T(8,128)(2,1)S(1)}, bf16[16,24,128]{2,1,0:T(8,128)(2,1)S(1)}, u32[]{:S(2)}, u32[]{:S(2)}) collective-permute-start(bf16[16,24,128]{2,1,0:T(8,128)(2,1)S(1)} %get-tuple-element.28.high), channel_id=1, source_target_pairs={{0,24},{8,16},{16,8},{24,0},{1,25},{9,17},{17,9},{25,1},{2,26},{10... | collective-permute-start | bytes 294920 | tf_op jit(solution)/shard_map/ppermute | solution.py:43
  19.7 6.3 %collective-permute-start.4 = (bf16[16,24,128]{2,1,0:T(8,128)(2,1)S(1)}, bf16[16,24,128]{2,1,0:T(8,128)(2,1)S(1)}, u32[]{:S(2)}, u32[]{:S(2)}) collective-permute-start(bf16[16,24,128]{2,1,0:T(8,128)(2,1)S(1)} %get-tuple-element.28.high), channel_id=1, source_target_pairs={{0,8},{8,0},{16,24},{24,16},{1,9},{9,1},{17,25},{25,17},{2,10},{10... | collective-permute-start | bytes 294920 | tf_op jit(solution)/shard_map/ppermute | solution.py:46
  26.6 7.5 %collective-permute-start.11 = (bf16[16,24,128]{2,1,0:T(8,128)(2,1)S(1)}, bf16[16,24,128]{2,1,0:T(8,128)(2,1)S(1)}, u32[]{:S(2)}, u32[]{:S(2)}) collective-permute-start(bf16[16,24,128]{2,1,0:T(8,128)(2,1)S(1)} %get-tuple-element.33.high), channel_id=1, source_target_pairs={{0,7},{1,2},{2,1},{3,4},{4,3},{5,6},{6,5},{7,0},{8,15},{9,10},{10,... | collective-permute-start | bytes 294920 | tf_op jit(solution)/shard_map/ppermute | solution.py:44
  29.4 5.6 %collective-permute-start.10 = (bf16[16,24,128]{2,1,0:T(8,128)(2,1)S(1)}, bf16[16,24,128]{2,1,0:T(8,128)(2,1)S(1)}, u32[]{:S(2)}, u32[]{:S(2)}) collective-permute-start(bf16[16,24,128]{2,1,0:T(8,128)(2,1)S(1)} %get-tuple-element.33.high), channel_id=1, source_target_pairs={{0,1},{1,0},{2,3},{3,2},{4,5},{5,4},{6,7},{7,6},{8,9},{9,8},{10,11... | collective-permute-start | bytes 294920 | tf_op jit(solution)/shard_map/ppermute | solution.py:45
  29.4 5.6 %collective-permute-start.9 = (bf16[16,24,128]{2,1,0:T(8,128)(2,1)S(1)}, bf16[16,24,128]{2,1,0:T(8,128)(2,1)S(1)}, u32[]{:S(2)}, u32[]{:S(2)}) collective-permute-start(bf16[16,24,128]{2,1,0:T(8,128)(2,1)S(1)} %get-tuple-element.33.high), channel_id=1, source_target_pairs={{0,24},{8,16},{16,8},{24,0},{1,25},{9,17},{17,9},{25,1},{2,26},{10... | collective-permute-start | bytes 294920 | tf_op jit(solution)/shard_map/ppermute | solution.py:43
  29.4 5.6 %collective-permute-start.8 = (bf16[16,24,128]{2,1,0:T(8,128)(2,1)S(1)}, bf16[16,24,128]{2,1,0:T(8,128)(2,1)S(1)}, u32[]{:S(2)}, u32[]{:S(2)}) collective-permute-start(bf16[16,24,128]{2,1,0:T(8,128)(2,1)S(1)} %get-tuple-element.33.high), channel_id=1, source_target_pairs={{0,8},{8,0},{16,24},{24,16},{1,9},{9,1},{17,25},{25,17},{2,10},{10... | collective-permute-start | bytes 294920 | tf_op jit(solution)/shard_map/ppermute | solution.py:46

commit v4 on v3

--- a/solution.py
+++ b/solution.py
@@ -22,8 +22,8 @@
 PARAMS = pltpu.CompilerParams(vmem_limit_bytes=LIMIT)
 
 
-def pairings(count):
-    if count % 2:
+def pairings(count, ring=False):
+    if ring or count % 2:
         ahead = [(i, (i - 1) % count) for i in range(count)]
         return ahead, [(target, source) for source, target in ahead]
     first = [(i, i ^ 1) for i in range(count)]
@@ -39,12 +39,12 @@
 
 def exchange(high):
     z_first, z_second = pairings(lax.axis_size("dev"))
-    t_first, t_second = pairings(lax.axis_size("grp"))
+    t_first, t_second = pairings(lax.axis_size("grp"), True)
     t_two = lax.ppermute(high, "grp", t_second)
     z_two = lax.ppermute(high, "dev", z_second)
     z_one = lax.ppermute(high, "dev", z_first)
     t_one = lax.ppermute(high, "grp", t_first)
-    return t_one, t_two, z_one, z_two
+    return t_two, t_one, z_one, z_two
 
 
 def lanes(shape):
@@ -231,8 +231,8 @@
     return part[s] + joined(product, rows) - SHIFT * before[s]
 
 
-def halo_kernel(t_one, t_two, z_one, z_two, part, before, oper_ref, value_ref, high_ref, low_ref):
-    flips = (swapped("grp"), swapped("dev"))
+def halo_kernel(t_two, t_one, z_one, z_two, part, before, oper_ref, value_ref, high_ref, low_ref):
+    flips = (jnp.bool_(False), swapped("dev"))
     for s in range(part.shape[0]):
         value = halo_value(s, flips, ((t_one, t_two), (z_one, z_two)), part, before, oper_ref)
         value_ref[s] = value
@@ -267,8 +267,8 @@
     return packed
 
 
-def last_kernel(t_one, t_two, z_one, z_two, part, r0, v1, w1, v2, w2, early, oper_ref, v3, sums_ref):
-    flips = (swapped("grp"), swapped("dev"))
+def last_kernel(t_two, t_one, z_one, z_two, part, r0, v1, w1, v2, w2, early, oper_ref, v3, sums_ref):
+    flips = (jnp.bool_(False), swapped("dev"))
     sites, rows, wide = part.shape
     for s in range(sites):
         v3[s] = halo_value(s, flips, ((t_one, t_two), (z_one, z_two)), part, v2, oper_ref)

time: 49.9 us -> 49.6 us (level)
  starting transfers between devices: 15.2 us -> 12.7 us
  waiting for transfers between devices: 8.85 us -> 11.3 us
    ppermute x3, starting transfers between devices: 3.34 us -> 0.66 us  [exchange(): t_one = lax.ppermute(high, 'grp', t_first)]
    ppermute x3, waiting for transfers between devices: 5.84 us -> 7.21 us  [exchange(): z_two = lax.ppermute(high, 'dev', z_second)]
    ppermute x3, waiting for transfers between devices: 2.84 us -> 3.8 us  [exchange(): z_one = lax.ppermute(high, 'dev', z_first)]
where the time goes in v4:
time: 49.6 us; the launch traced here: 49.4 us
  Pallas kernels  14.3 us (29%)
  starting transfers between devices  12.7 us (26%)
  waiting for transfers between devices  11.3 us (23%)
  blocking collectives  10.5 us (21%)
  between operations  0.69 us (1%)
    ppermute x3, starting transfers between devices, exchange(): z_two = lax.ppermute(high, 'dev', z_second)  11 us
    all_to_all x1, blocking collectives, on_device(): sums = lax.all_to_all(sums, ('grp', 'dev'), 0, 0)  10.5 us
    ppermute x3, waiting for transfers between devices, exchange(): z_two = lax.ppermute(high, 'dev', z_second)  7.21 us
    pallas_call x1, Pallas kernels, restrict(): pl.pallas_call(restrict_kernel, in_specs=[HBM] * 2, out_specs=[VM] * 4, o...  4.98 us
    ppermute x3, waiting for transfers between devices, exchange(): z_one = lax.ppermute(high, 'dev', z_first)  3.8 us
    pallas_call x1, Pallas kernels, finish(): pl.pallas_call(finish_kernel, in_specs=[VM] * 8, out_specs=[HBM, HBM], ou...  3.25 us
    pallas_call x1, Pallas kernels, on_device(): pl.pallas_call(functools.partial(first_local_kernel, dims), in_specs=[VM,...  2.37 us
    pallas_call x2, Pallas kernels, on_device(): pl.pallas_call(halo_kernel, in_specs=[VM] * 7, out_specs=[VM] * 3, out_sh...  1.1 us
  transfers between devices with their start and end apart: 12, of which 6 were waited for; matrix products, arithmetic and copies ran while one was open for 0% of the time, Pallas kernels for 8%

profile of v4, /device:TPU:0, one launch (start us, length us, event | category | flops | bytes accessed | tf_op | source)
XLA Modules:
  0.0 49.4 jit_solution(11893544022418889531)
XLA Ops:
  0.6 5.0 %restrict.1 = (f32[16,24,128]{2,1,0:T(8,128)S(1)}, bf16[16,24,128]{2,1,0:T(8,128)(2,1)S(1)}, bf16[16,24,128]{2,1,0:T(8,128)(2,1)S(1)}, bf16[16,64,3072]{2,1,0:T(8,128)(2,1)S(1)}) custom-call(bf16[16,24,2,3072]{3,2,1,0:T(2,128)(2,1)} %bitcast.7, bf16[16,64,3072]{2,1,0:T(8,128)(2,1)} %bitcast.6), custom_call_target="tpu_custom_call" | custom-call | tf_op jit(solution)/shard_map/restrict/pallas_call | solution.py:140
  5.6 6.1 %collective-permute-start.3 = (bf16[16,24,128]{2,1,0:T(8,128)(2,1)S(1)}, bf16[16,24,128]{2,1,0:T(8,128)(2,1)S(1)}, u32[]{:S(2)}, u32[]{:S(2)}) collective-permute-start(bf16[16,24,128]{2,1,0:T(8,128)(2,1)S(1)} %get-tuple-element.23.high), channel_id=1, source_target_pairs={{0,7},{1,2},{2,1},{3,4},{4,3},{5,6},{6,5},{7,0},{8,15},{9,10},{10,... | collective-permute-start | bytes 294920 | tf_op jit(solution)/shard_map/ppermute | solution.py:44
  11.7 0.7 %collective-permute-start.1 = (bf16[16,24,128]{2,1,0:T(8,128)(2,1)S(1)}, bf16[16,24,128]{2,1,0:T(8,128)(2,1)S(1)}, u32[]{:S(2)}, u32[]{:S(2)}) collective-permute-start(bf16[16,24,128]{2,1,0:T(8,128)(2,1)S(1)} %get-tuple-element.23.high), channel_id=1, source_target_pairs={{0,24},{8,0},{16,8},{24,16},{1,25},{9,1},{17,9},{25,17},{2,26},{10... | collective-permute-start | bytes 294920 | tf_op jit(solution)/shard_map/ppermute | solution.py:46
  12.3 0.0 collective-permute-start
  12.3 2.4 %local_1.1 = (f32[16,24,128]{2,1,0:T(8,128)S(1)}, f32[16,24,128]{2,1,0:T(8,128)S(1)}, bf16[16,64,1152]{2,1,0:T(8,128)(2,1)S(1)}) custom-call(bf16[16,24,128]{2,1,0:T(8,128)(2,1)S(1)} %get-tuple-element.23.high, bf16[16,24,128]{2,1,0:T(8,128)(2,1)S(1)} %get-tuple-element.24.low, bf16[4,16,64,1152]{3,2,1,0:T(8,128)(2,1)} %bitcast.5), custom_call_target="tpu_custom_call" | custom-call | tf_op jit(solution)/shard_map/local_1/pallas_call | solution.py:504
  14.7 1.8 %collective-permute-done.2.z_one = bf16[16,24,128]{2,1,0:T(8,128)(2,1)S(1)} collective-permute-done((bf16[16,24,128]{2,1,0:T(8,128)(2,1)S(1)}, bf16[16,24,128]{2,1,0:T(8,128)(2,1)S(1)}, u32[]{:S(2)}, u32[]{:S(2)}) %collective-permute-start.2) | collective-permute-done | bytes 98336 | tf_op jit(solution)/shard_map/ppermute | solution.py:45
  16.6 0.0 collective-permute-done.1.t_one
  16.6 0.2 collective-permute-done.t_two
  16.8 0.6 %halo_1.1 = (f32[16,24,128]{2,1,0:T(8,128)S(1)}, bf16[16,24,128]{2,1,0:T(8,128)(2,1)S(1)}, bf16[16,24,128]{2,1,0:T(8,128)(2,1)S(1)}) custom-call(bf16[16,24,128]{2,1,0:T(8,128)(2,1)S(1)} %collective-permute-done.t_two, bf16[16,24,128]{2,1,0:T(8,128)(2,1)S(1)} %collective-permute-done.1.t_one, bf16[16,24,128]{2,1,0:T(8,128)(2,1)S(1)} %collective-permute-done.2.z_one, ...), custom_call_target="tpu_custom_call" | custom-call | tf_op jit(solution)/shard_map/halo_1/pallas_call | solution.py:513
  17.4 2.3 %collective-permute-start.7 = (bf16[16,24,128]{2,1,0:T(8,128)(2,1)S(1)}, bf16[16,24,128]{2,1,0:T(8,128)(2,1)S(1)}, u32[]{:S(2)}, u32[]{:S(2)}) collective-permute-start(bf16[16,24,128]{2,1,0:T(8,128)(2,1)S(1)} %get-tuple-element.28.high), channel_id=1, source_target_pairs={{0,7},{1,2},{2,1},{3,4},{4,3},{5,6},{6,5},{7,0},{8,15},{9,10},{10,... | collective-permute-start | bytes 294920 | tf_op jit(solution)/shard_map/ppermute | solution.py:44
  19.6 0.5 %collective-permute-start.4 = (bf16[16,24,128]{2,1,0:T(8,128)(2,1)S(1)}, bf16[16,24,128]{2,1,0:T(8,128)(2,1)S(1)}, u32[]{:S(2)}, u32[]{:S(2)}) collective-permute-start(bf16[16,24,128]{2,1,0:T(8,128)(2,1)S(1)} %get-tuple-element.28.high), channel_id=1, source_target_pairs={{24,0},{0,8},{8,16},{16,24},{25,1},{1,9},{9,17},{17,25},{26,2},{2,... | collective-permute-start | bytes 294920 | tf_op jit(solution)/shard_map/ppermute | solution.py:43
  20.2 0.9 %local_2.1 = (f32[16,24,128]{2,1,0:T(8,128)S(1)}, f32[16,24,128]{2,1,0:T(8,128)S(1)}) custom-call(bf16[16,24,128]{2,1,0:T(8,128)(2,1)S(1)} %get-tuple-element.28.high, bf16[16,24,128]{2,1,0:T(8,128)(2,1)S(1)} %get-tuple-element.29.low, f32[16,24,128]{2,1,0:T(8,128)S(1)} %get-tuple-element.30.rest.w1, bf16[16,64,1152]{2,1,0:T(8,128)(2,1)S(1)} %get-tuple-element.27.oper_ref), custom_call_target="tpu_custom_call" | custom-call | tf_op jit(solution)/shard_map/local_2/pallas_call | solution.py:523
  21.0 3.8 %collective-permute-done.7.z_two = bf16[16,24,128]{2,1,0:T(8,128)(2,1)S(1)} collective-permute-done((bf16[16,24,128]{2,1,0:T(8,128)(2,1)S(1)}, bf16[16,24,128]{2,1,0:T(8,128)(2,1)S(1)}, u32[]{:S(2)}, u32[]{:S(2)}) %collective-permute-start.7) | collective-permute-done | bytes 98336 | tf_op jit(solution)/shard_map/ppermute | solution.py:44
  24.8 0.8 %collective-permute-done.6.z_one = bf16[16,24,128]{2,1,0:T(8,128)(2,1)S(1)} collective-permute-done((bf16[16,24,128]{2,1,0:T(8,128)(2,1)S(1)}, bf16[16,24,128]{2,1,0:T(8,128)(2,1)S(1)}, u32[]{:S(2)}, u32[]{:S(2)}) %collective-permute-start.6) | collective-permute-done | bytes 98336 | tf_op jit(solution)/shard_map/ppermute | solution.py:45
  25.7 0.6 %halo_2.1 = (f32[16,24,128]{2,1,0:T(8,128)S(1)}, bf16[16,24,128]{2,1,0:T(8,128)(2,1)S(1)}, bf16[16,24,128]{2,1,0:T(8,128)(2,1)S(1)}) custom-call(bf16[16,24,128]{2,1,0:T(8,128)(2,1)S(1)} %collective-permute-done.4.t_two, bf16[16,24,128]{2,1,0:T(8,128)(2,1)S(1)} %collective-permute-done.5.t_one, bf16[16,24,128]{2,1,0:T(8,128)(2,1)S(1)} %collective-permute-done.6.z_one, ...), custom_call_target="tpu_custom_call" | custom-call | tf_op jit(solution)/shard_map/halo_2/pallas_call | solution.py:532
  26.2 2.7 %collective-permute-start.11 = (bf16[16,24,128]{2,1,0:T(8,128)(2,1)S(1)}, bf16[16,24,128]{2,1,0:T(8,128)(2,1)S(1)}, u32[]{:S(2)}, u32[]{:S(2)}) collective-permute-start(bf16[16,24,128]{2,1,0:T(8,128)(2,1)S(1)} %get-tuple-element.33.high), channel_id=1, source_target_pairs={{0,7},{1,2},{2,1},{3,4},{4,3},{5,6},{6,5},{7,0},{8,15},{9,10},{10,... | collective-permute-start | bytes 294920 | tf_op jit(solution)/shard_map/ppermute | solution.py:44
  28.9 0.5 %collective-permute-start.8 = (bf16[16,24,128]{2,1,0:T(8,128)(2,1)S(1)}, bf16[16,24,128]{2,1,0:T(8,128)(2,1)S(1)}, u32[]{:S(2)}, u32[]{:S(2)}) collective-permute-start(bf16[16,24,128]{2,1,0:T(8,128)(2,1)S(1)} %get-tuple-element.33.high), channel_id=1, source_target_pairs={{24,0},{0,8},{8,16},{16,24},{25,1},{1,9},{9,17},{17,25},{26,2},{2,... | collective-permute-start | bytes 294920 | tf_op jit(solution)/shard_map/ppermute | solution.py:43
  29.4 0.9 %local_3.1 = (f32[16,24,128]{2,1,0:T(8,128)S(1)}, f32[24,128]{1,0:T(8,128)S(1)}) custom-call(bf16[16,24,128]{2,1,0:T(8,128)(2,1)S(1)} %get-tuple-element.33.high, bf16[16,24,128]{2,1,0:T(8,128)(2,1)S(1)} %get-tuple-element.34.low, f32[16,24,128]{2,1,0:T(8,128)S(1)} %get-tuple-element.26.before.r0, f32[16,24,128]{2,1,0:T(8,128)S(1)} %get-tuple-element.32.before.v1, ...), custom_call_target="tpu_custom_call" | custom-call | tf_op jit(solution)/shard_map/local_3/pallas_call | solution.py:542
  30.3 3.4 %collective-permute-done.11.z_two = bf16[16,24,128]{2,1,0:T(8,128)(2,1)S(1)} collective-permute-done((bf16[16,24,128]{2,1,0:T(8,128)(2,1)S(1)}, bf16[16,24,128]{2,1,0:T(8,128)(2,1)S(1)}, u32[]{:S(2)}, u32[]{:S(2)}) %collective-permute-start.11) | collective-permute-done | bytes 98336 | tf_op jit(solution)/shard_map/ppermute | solution.py:44
  33.7 1.1 %collective-permute-done.10.z_one = bf16[16,24,128]{2,1,0:T(8,128)(2,1)S(1)} collective-permute-done((bf16[16,24,128]{2,1,0:T(8,128)(2,1)S(1)}, bf16[16,24,128]{2,1,0:T(8,128)(2,1)S(1)}, u32[]{:S(2)}, u32[]{:S(2)}) %collective-permute-start.10) | collective-permute-done | bytes 98336 | tf_op jit(solution)/shard_map/ppermute | solution.py:45
  34.8 0.0 collective-permute-done.9.t_one
  34.8 0.9 %halo_3.1 = (f32[16,24,128]{2,1,0:T(8,128)S(1)}, f32[32,8,128]{2,1,0:T(8,128)S(1)}) custom-call(bf16[16,24,128]{2,1,0:T(8,128)(2,1)S(1)} %collective-permute-done.8.t_two, bf16[16,24,128]{2,1,0:T(8,128)(2,1)S(1)} %collective-permute-done.9.t_one, bf16[16,24,128]{2,1,0:T(8,128)(2,1)S(1)} %collective-permute-done.10.z_one, ...), custom_call_target="tpu_custom_call" | custom-call | tf_op jit(solution)/shard_map/halo_3/pallas_call | solution.py:552
  35.7 10.5 %all_to_all.5.sums = f32[32,8,128]{2,1,0:T(8,128)S(1)} all-to-all(f32[32,8,128]{2,1,0:T(8,128)S(1)} %get-tuple-element.39), channel_id=1, replica_groups=mesh['grp'=4,'dev'=8] {'grp','dev'}, dimensions={0} | all-to-all | bytes 262144 | tf_op jit(solution)/shard_map/all_to_all | solution.py:561
  46.2 3.2 %finish.1 = (bf16[16,24,2,3072]{3,2,1,0:T(2,128)(2,1)}, f32[16,24,128]{2,1,0:T(8,128)}) custom-call(f32[32,8,128]{2,1,0:T(8,128)S(1)} %all_to_all.5.sums, f32[16,24,128]{2,1,0:T(8,128)S(1)} %get-tuple-element.26.before.r0, f32[16,24,128]{2,1,0:T(8,128)S(1)} %get-tuple-element.32.before.v1, f32[16,24,128]{2,1,0:T(8,128)S(1)} %get-tuple-element.30.rest.w1, ...), custom_call_target="tpu_custom_call" | custom-call | tf_op jit(solution)/shard_map/finish/pallas_call | solution.py:469
  (9 shorter events, 0.0 us)
Async XLA Ops:
  5.6 9.1 %collective-permute-start.3 = (bf16[16,24,128]{2,1,0:T(8,128)(2,1)S(1)}, bf16[16,24,128]{2,1,0:T(8,128)(2,1)S(1)}, u32[]{:S(2)}, u32[]{:S(2)}) collective-permute-start(bf16[16,24,128]{2,1,0:T(8,128)(2,1)S(1)} %get-tuple-element.23.high), channel_id=1, source_target_pairs={{0,7},{1,2},{2,1},{3,4},{4,3},{5,6},{6,5},{7,0},{8,15},{9,10},{10,... | collective-permute-start | bytes 294920 | tf_op jit(solution)/shard_map/ppermute | solution.py:44
  11.7 4.9 %collective-permute-start.2 = (bf16[16,24,128]{2,1,0:T(8,128)(2,1)S(1)}, bf16[16,24,128]{2,1,0:T(8,128)(2,1)S(1)}, u32[]{:S(2)}, u32[]{:S(2)}) collective-permute-start(bf16[16,24,128]{2,1,0:T(8,128)(2,1)S(1)} %get-tuple-element.23.high), channel_id=1, source_target_pairs={{0,1},{1,0},{2,3},{3,2},{4,5},{5,4},{6,7},{7,6},{8,9},{9,8},{10,11... | collective-permute-start | bytes 294920 | tf_op jit(solution)/shard_map/ppermute | solution.py:45
  11.7 4.9 %collective-permute-start.1 = (bf16[16,24,128]{2,1,0:T(8,128)(2,1)S(1)}, bf16[16,24,128]{2,1,0:T(8,128)(2,1)S(1)}, u32[]{:S(2)}, u32[]{:S(2)}) collective-permute-start(bf16[16,24,128]{2,1,0:T(8,128)(2,1)S(1)} %get-tuple-element.23.high), channel_id=1, source_target_pairs={{0,24},{8,0},{16,8},{24,16},{1,25},{9,1},{17,9},{25,17},{2,26},{10... | collective-permute-start | bytes 294920 | tf_op jit(solution)/shard_map/ppermute | solution.py:46
  12.3 4.5 %collective-permute-start = (bf16[16,24,128]{2,1,0:T(8,128)(2,1)S(1)}, bf16[16,24,128]{2,1,0:T(8,128)(2,1)S(1)}, u32[]{:S(2)}, u32[]{:S(2)}) collective-permute-start(bf16[16,24,128]{2,1,0:T(8,128)(2,1)S(1)} %get-tuple-element.23.high), channel_id=1, source_target_pairs={{24,0},{0,8},{8,16},{16,24},{25,1},{1,9},{9,17},{17,25},{26,2},{2,... | collective-permute-start | bytes 294920 | tf_op jit(solution)/shard_map/ppermute | solution.py:43
  17.4 7.4 %collective-permute-start.7 = (bf16[16,24,128]{2,1,0:T(8,128)(2,1)S(1)}, bf16[16,24,128]{2,1,0:T(8,128)(2,1)S(1)}, u32[]{:S(2)}, u32[]{:S(2)}) collective-permute-start(bf16[16,24,128]{2,1,0:T(8,128)(2,1)S(1)} %get-tuple-element.28.high), channel_id=1, source_target_pairs={{0,7},{1,2},{2,1},{3,4},{4,3},{5,6},{6,5},{7,0},{8,15},{9,10},{10,... | collective-permute-start | bytes 294920 | tf_op jit(solution)/shard_map/ppermute | solution.py:44
  19.6 6.0 %collective-permute-start.6 = (bf16[16,24,128]{2,1,0:T(8,128)(2,1)S(1)}, bf16[16,24,128]{2,1,0:T(8,128)(2,1)S(1)}, u32[]{:S(2)}, u32[]{:S(2)}) collective-permute-start(bf16[16,24,128]{2,1,0:T(8,128)(2,1)S(1)} %get-tuple-element.28.high), channel_id=1, source_target_pairs={{0,1},{1,0},{2,3},{3,2},{4,5},{5,4},{6,7},{7,6},{8,9},{9,8},{10,11... | collective-permute-start | bytes 294920 | tf_op jit(solution)/shard_map/ppermute | solution.py:45
  19.6 6.0 %collective-permute-start.5 = (bf16[16,24,128]{2,1,0:T(8,128)(2,1)S(1)}, bf16[16,24,128]{2,1,0:T(8,128)(2,1)S(1)}, u32[]{:S(2)}, u32[]{:S(2)}) collective-permute-start(bf16[16,24,128]{2,1,0:T(8,128)(2,1)S(1)} %get-tuple-element.28.high), channel_id=1, source_target_pairs={{0,24},{8,0},{16,8},{24,16},{1,25},{9,1},{17,9},{25,17},{2,26},{10... | collective-permute-start | bytes 294920 | tf_op jit(solution)/shard_map/ppermute | solution.py:46
  19.6 6.0 %collective-permute-start.4 = (bf16[16,24,128]{2,1,0:T(8,128)(2,1)S(1)}, bf16[16,24,128]{2,1,0:T(8,128)(2,1)S(1)}, u32[]{:S(2)}, u32[]{:S(2)}) collective-permute-start(bf16[16,24,128]{2,1,0:T(8,128)(2,1)S(1)} %get-tuple-element.28.high), channel_id=1, source_target_pairs={{24,0},{0,8},{8,16},{16,24},{25,1},{1,9},{9,17},{17,25},{26,2},{2,... | collective-permute-start | bytes 294920 | tf_op jit(solution)/shard_map/ppermute | solution.py:43
  26.2 7.5 %collective-permute-start.11 = (bf16[16,24,128]{2,1,0:T(8,128)(2,1)S(1)}, bf16[16,24,128]{2,1,0:T(8,128)(2,1)S(1)}, u32[]{:S(2)}, u32[]{:S(2)}) collective-permute-start(bf16[16,24,128]{2,1,0:T(8,128)(2,1)S(1)} %get-tuple-element.33.high), channel_id=1, source_target_pairs={{0,7},{1,2},{2,1},{3,4},{4,3},{5,6},{6,5},{7,0},{8,15},{9,10},{10,... | collective-permute-start | bytes 294920 | tf_op jit(solution)/shard_map/ppermute | solution.py:44
  28.9 5.9 %collective-permute-start.10 = (bf16[16,24,128]{2,1,0:T(8,128)(2,1)S(1)}, bf16[16,24,128]{2,1,0:T(8,128)(2,1)S(1)}, u32[]{:S(2)}, u32[]{:S(2)}) collective-permute-start(bf16[16,24,128]{2,1,0:T(8,128)(2,1)S(1)} %get-tuple-element.33.high), channel_id=1, source_target_pairs={{0,1},{1,0},{2,3},{3,2},{4,5},{5,4},{6,7},{7,6},{8,9},{9,8},{10,11... | collective-permute-start | bytes 294920 | tf_op jit(solution)/shard_map/ppermute | solution.py:45
  28.9 5.9 %collective-permute-start.9 = (bf16[16,24,128]{2,1,0:T(8,128)(2,1)S(1)}, bf16[16,24,128]{2,1,0:T(8,128)(2,1)S(1)}, u32[]{:S(2)}, u32[]{:S(2)}) collective-permute-start(bf16[16,24,128]{2,1,0:T(8,128)(2,1)S(1)} %get-tuple-element.33.high), channel_id=1, source_target_pairs={{0,24},{8,0},{16,8},{24,16},{1,25},{9,1},{17,9},{25,17},{2,26},{10... | collective-permute-start | bytes 294920 | tf_op jit(solution)/shard_map/ppermute | solution.py:46
  28.9 5.9 %collective-permute-start.8 = (bf16[16,24,128]{2,1,0:T(8,128)(2,1)S(1)}, bf16[16,24,128]{2,1,0:T(8,128)(2,1)S(1)}, u32[]{:S(2)}, u32[]{:S(2)}) collective-permute-start(bf16[16,24,128]{2,1,0:T(8,128)(2,1)S(1)} %get-tuple-element.33.high), channel_id=1, source_target_pairs={{24,0},{0,8},{8,16},{16,24},{25,1},{1,9},{9,17},{17,25},{26,2},{2,... | collective-permute-start | bytes 294920 | tf_op jit(solution)/shard_map/ppermute | solution.py:43

commit v5 on v4

--- a/solution.py
+++ b/solution.py
@@ -249,12 +249,12 @@
     return table
 
 
-def inner_sums(basis, table):
+def inner_sums(basis, table, newest=None):
     sites, rows, wide = basis[0].shape
     half = wide // 2
     total = {key: jnp.zeros((rows, wide), F32) for key in table}
     for s in range(sites):
-        plain = [b[s] for b in basis]
+        plain = [b[s] for b in basis] + ([newest(s)] if newest else [])
         turned = {j: pltpu.roll(plain[j], half, 1) for j in sorted({k[1] for k in table if k[2]})}
         for i, j, imaginary in table:
             total[(i, j, imaginary)] += plain[i] * (turned[j] if imaginary else plain[j])
@@ -270,10 +270,14 @@
 def last_kernel(t_two, t_one, z_one, z_two, part, r0, v1, w1, v2, w2, early, oper_ref, v3, sums_ref):
     flips = (jnp.bool_(False), swapped("dev"))
     sites, rows, wide = part.shape
-    for s in range(sites):
-        v3[s] = halo_value(s, flips, ((t_one, t_two), (z_one, z_two)), part, v2, oper_ref)
     table = slots(BASIS)
-    late = inner_sums([r0, v1, w1, v2, w2, v3], {k: i for k, i in table.items() if k[1] == BASIS - 1})
+
+    def newest(s):
+        value = halo_value(s, flips, ((t_one, t_two), (z_one, z_two)), part, v2, oper_ref)
+        v3[s] = value
+        return value
+
+    late = inner_sums([r0, v1, w1, v2, w2], {k: i for k, i in table.items() if k[1] == BASIS - 1}, newest)
     packed = early[...] + late
     square = packed.T
     groups = -(-len(table) // 8)

time: 49.6 us -> 49.6 us (level)
  no operation moved by 1% of the time
where the time goes in v5:
time: 49.6 us; the launch traced here: 49.4 us
  Pallas kernels  14.3 us (29%)
  starting transfers between devices  12.7 us (26%)
  waiting for transfers between devices  11.3 us (23%)
  blocking collectives  10.5 us (21%)
  between operations  0.69 us (1%)
    ppermute x3, starting transfers between devices, exchange(): z_two = lax.ppermute(high, 'dev', z_second)  11 us
    all_to_all x1, blocking collectives, on_device(): sums = lax.all_to_all(sums, ('grp', 'dev'), 0, 0)  10.5 us
    ppermute x3, waiting for transfers between devices, exchange(): z_two = lax.ppermute(high, 'dev', z_second)  7.21 us
    pallas_call x1, Pallas kernels, restrict(): pl.pallas_call(restrict_kernel, in_specs=[HBM] * 2, out_specs=[VM] * 4, o...  4.98 us
    ppermute x3, waiting for transfers between devices, exchange(): z_one = lax.ppermute(high, 'dev', z_first)  3.8 us
    pallas_call x1, Pallas kernels, finish(): pl.pallas_call(finish_kernel, in_specs=[VM] * 8, out_specs=[HBM, HBM], ou...  3.25 us
    pallas_call x1, Pallas kernels, on_device(): pl.pallas_call(functools.partial(first_local_kernel, dims), in_specs=[VM,...  2.37 us
    pallas_call x2, Pallas kernels, on_device(): pl.pallas_call(halo_kernel, in_specs=[VM] * 7, out_specs=[VM] * 3, out_sh...  1.1 us
  transfers between devices with their start and end apart: 12, of which 6 were waited for; matrix products, arithmetic and copies ran while one was open for 0% of the time, Pallas kernels for 8%

profile of v5, /device:TPU:0, one launch (start us, length us, event | category | flops | bytes accessed | tf_op | source)
XLA Modules:
  0.0 49.4 jit_solution(4712939911681519113)
XLA Ops:
  0.6 5.0 %restrict.1 = (f32[16,24,128]{2,1,0:T(8,128)S(1)}, bf16[16,24,128]{2,1,0:T(8,128)(2,1)S(1)}, bf16[16,24,128]{2,1,0:T(8,128)(2,1)S(1)}, bf16[16,64,3072]{2,1,0:T(8,128)(2,1)S(1)}) custom-call(bf16[16,24,2,3072]{3,2,1,0:T(2,128)(2,1)} %bitcast.7, bf16[16,64,3072]{2,1,0:T(8,128)(2,1)} %bitcast.6), custom_call_target="tpu_custom_call" | custom-call | tf_op jit(solution)/shard_map/restrict/pallas_call | solution.py:140
  5.6 6.1 %collective-permute-start.3 = (bf16[16,24,128]{2,1,0:T(8,128)(2,1)S(1)}, bf16[16,24,128]{2,1,0:T(8,128)(2,1)S(1)}, u32[]{:S(2)}, u32[]{:S(2)}) collective-permute-start(bf16[16,24,128]{2,1,0:T(8,128)(2,1)S(1)} %get-tuple-element.23.high), channel_id=1, source_target_pairs={{0,7},{1,2},{2,1},{3,4},{4,3},{5,6},{6,5},{7,0},{8,15},{9,10},{10,... | collective-permute-start | bytes 294920 | tf_op jit(solution)/shard_map/ppermute | solution.py:44
  11.7 0.7 %collective-permute-start.1 = (bf16[16,24,128]{2,1,0:T(8,128)(2,1)S(1)}, bf16[16,24,128]{2,1,0:T(8,128)(2,1)S(1)}, u32[]{:S(2)}, u32[]{:S(2)}) collective-permute-start(bf16[16,24,128]{2,1,0:T(8,128)(2,1)S(1)} %get-tuple-element.23.high), channel_id=1, source_target_pairs={{0,24},{8,0},{16,8},{24,16},{1,25},{9,1},{17,9},{25,17},{2,26},{10... | collective-permute-start | bytes 294920 | tf_op jit(solution)/shard_map/ppermute | solution.py:46
  12.3 0.0 collective-permute-start
  12.3 2.4 %local_1.1 = (f32[16,24,128]{2,1,0:T(8,128)S(1)}, f32[16,24,128]{2,1,0:T(8,128)S(1)}, bf16[16,64,1152]{2,1,0:T(8,128)(2,1)S(1)}) custom-call(bf16[16,24,128]{2,1,0:T(8,128)(2,1)S(1)} %get-tuple-element.23.high, bf16[16,24,128]{2,1,0:T(8,128)(2,1)S(1)} %get-tuple-element.24.low, bf16[4,16,64,1152]{3,2,1,0:T(8,128)(2,1)} %bitcast.5), custom_call_target="tpu_custom_call" | custom-call | tf_op jit(solution)/shard_map/local_1/pallas_call | solution.py:508
  14.7 1.8 %collective-permute-done.2.z_one = bf16[16,24,128]{2,1,0:T(8,128)(2,1)S(1)} collective-permute-done((bf16[16,24,128]{2,1,0:T(8,128)(2,1)S(1)}, bf16[16,24,128]{2,1,0:T(8,128)(2,1)S(1)}, u32[]{:S(2)}, u32[]{:S(2)}) %collective-permute-start.2) | collective-permute-done | bytes 98336 | tf_op jit(solution)/shard_map/ppermute | solution.py:45
  16.6 0.0 collective-permute-done.1.t_one
  16.6 0.2 collective-permute-done.t_two
  16.8 0.6 %halo_1.1 = (f32[16,24,128]{2,1,0:T(8,128)S(1)}, bf16[16,24,128]{2,1,0:T(8,128)(2,1)S(1)}, bf16[16,24,128]{2,1,0:T(8,128)(2,1)S(1)}) custom-call(bf16[16,24,128]{2,1,0:T(8,128)(2,1)S(1)} %collective-permute-done.t_two, bf16[16,24,128]{2,1,0:T(8,128)(2,1)S(1)} %collective-permute-done.1.t_one, bf16[16,24,128]{2,1,0:T(8,128)(2,1)S(1)} %collective-permute-done.2.z_one, ...), custom_call_target="tpu_custom_call" | custom-call | tf_op jit(solution)/shard_map/halo_1/pallas_call | solution.py:517
  17.4 2.3 %collective-permute-start.7 = (bf16[16,24,128]{2,1,0:T(8,128)(2,1)S(1)}, bf16[16,24,128]{2,1,0:T(8,128)(2,1)S(1)}, u32[]{:S(2)}, u32[]{:S(2)}) collective-permute-start(bf16[16,24,128]{2,1,0:T(8,128)(2,1)S(1)} %get-tuple-element.28.high), channel_id=1, source_target_pairs={{0,7},{1,2},{2,1},{3,4},{4,3},{5,6},{6,5},{7,0},{8,15},{9,10},{10,... | collective-permute-start | bytes 294920 | tf_op jit(solution)/shard_map/ppermute | solution.py:44
  19.6 0.5 %collective-permute-start.4 = (bf16[16,24,128]{2,1,0:T(8,128)(2,1)S(1)}, bf16[16,24,128]{2,1,0:T(8,128)(2,1)S(1)}, u32[]{:S(2)}, u32[]{:S(2)}) collective-permute-start(bf16[16,24,128]{2,1,0:T(8,128)(2,1)S(1)} %get-tuple-element.28.high), channel_id=1, source_target_pairs={{24,0},{0,8},{8,16},{16,24},{25,1},{1,9},{9,17},{17,25},{26,2},{2,... | collective-permute-start | bytes 294920 | tf_op jit(solution)/shard_map/ppermute | solution.py:43
  20.2 0.9 %local_2.1 = (f32[16,24,128]{2,1,0:T(8,128)S(1)}, f32[16,24,128]{2,1,0:T(8,128)S(1)}) custom-call(bf16[16,24,128]{2,1,0:T(8,128)(2,1)S(1)} %get-tuple-element.28.high, bf16[16,24,128]{2,1,0:T(8,128)(2,1)S(1)} %get-tuple-element.29.low, f32[16,24,128]{2,1,0:T(8,128)S(1)} %get-tuple-element.30.rest.w1, bf16[16,64,1152]{2,1,0:T(8,128)(2,1)S(1)} %get-tuple-element.27.oper_ref), custom_call_target="tpu_custom_call" | custom-call | tf_op jit(solution)/shard_map/local_2/pallas_call | solution.py:527
  21.0 3.8 %collective-permute-done.7.z_two = bf16[16,24,128]{2,1,0:T(8,128)(2,1)S(1)} collective-permute-done((bf16[16,24,128]{2,1,0:T(8,128)(2,1)S(1)}, bf16[16,24,128]{2,1,0:T(8,128)(2,1)S(1)}, u32[]{:S(2)}, u32[]{:S(2)}) %collective-permute-start.7) | collective-permute-done | bytes 98336 | tf_op jit(solution)/shard_map/ppermute | solution.py:44
  24.8 0.8 %collective-permute-done.6.z_one = bf16[16,24,128]{2,1,0:T(8,128)(2,1)S(1)} collective-permute-done((bf16[16,24,128]{2,1,0:T(8,128)(2,1)S(1)}, bf16[16,24,128]{2,1,0:T(8,128)(2,1)S(1)}, u32[]{:S(2)}, u32[]{:S(2)}) %collective-permute-start.6) | collective-permute-done | bytes 98336 | tf_op jit(solution)/shard_map/ppermute | solution.py:45
  25.7 0.6 %halo_2.1 = (f32[16,24,128]{2,1,0:T(8,128)S(1)}, bf16[16,24,128]{2,1,0:T(8,128)(2,1)S(1)}, bf16[16,24,128]{2,1,0:T(8,128)(2,1)S(1)}) custom-call(bf16[16,24,128]{2,1,0:T(8,128)(2,1)S(1)} %collective-permute-done.4.t_two, bf16[16,24,128]{2,1,0:T(8,128)(2,1)S(1)} %collective-permute-done.5.t_one, bf16[16,24,128]{2,1,0:T(8,128)(2,1)S(1)} %collective-permute-done.6.z_one, ...), custom_call_target="tpu_custom_call" | custom-call | tf_op jit(solution)/shard_map/halo_2/pallas_call | solution.py:536
  26.2 2.7 %collective-permute-start.11 = (bf16[16,24,128]{2,1,0:T(8,128)(2,1)S(1)}, bf16[16,24,128]{2,1,0:T(8,128)(2,1)S(1)}, u32[]{:S(2)}, u32[]{:S(2)}) collective-permute-start(bf16[16,24,128]{2,1,0:T(8,128)(2,1)S(1)} %get-tuple-element.33.high), channel_id=1, source_target_pairs={{0,7},{1,2},{2,1},{3,4},{4,3},{5,6},{6,5},{7,0},{8,15},{9,10},{10,... | collective-permute-start | bytes 294920 | tf_op jit(solution)/shard_map/ppermute | solution.py:44
  28.9 0.5 %collective-permute-start.8 = (bf16[16,24,128]{2,1,0:T(8,128)(2,1)S(1)}, bf16[16,24,128]{2,1,0:T(8,128)(2,1)S(1)}, u32[]{:S(2)}, u32[]{:S(2)}) collective-permute-start(bf16[16,24,128]{2,1,0:T(8,128)(2,1)S(1)} %get-tuple-element.33.high), channel_id=1, source_target_pairs={{24,0},{0,8},{8,16},{16,24},{25,1},{1,9},{9,17},{17,25},{26,2},{2,... | collective-permute-start | bytes 294920 | tf_op jit(solution)/shard_map/ppermute | solution.py:43
  29.4 0.9 %local_3.1 = (f32[16,24,128]{2,1,0:T(8,128)S(1)}, f32[24,128]{1,0:T(8,128)S(1)}) custom-call(bf16[16,24,128]{2,1,0:T(8,128)(2,1)S(1)} %get-tuple-element.33.high, bf16[16,24,128]{2,1,0:T(8,128)(2,1)S(1)} %get-tuple-element.34.low, f32[16,24,128]{2,1,0:T(8,128)S(1)} %get-tuple-element.26.before.r0, f32[16,24,128]{2,1,0:T(8,128)S(1)} %get-tuple-element.32.before.v1, ...), custom_call_target="tpu_custom_call" | custom-call | tf_op jit(solution)/shard_map/local_3/pallas_call | solution.py:546
  30.3 3.4 %collective-permute-done.11.z_two = bf16[16,24,128]{2,1,0:T(8,128)(2,1)S(1)} collective-permute-done((bf16[16,24,128]{2,1,0:T(8,128)(2,1)S(1)}, bf16[16,24,128]{2,1,0:T(8,128)(2,1)S(1)}, u32[]{:S(2)}, u32[]{:S(2)}) %collective-permute-start.11) | collective-permute-done | bytes 98336 | tf_op jit(solution)/shard_map/ppermute | solution.py:44
  33.7 1.1 %collective-permute-done.10.z_one = bf16[16,24,128]{2,1,0:T(8,128)(2,1)S(1)} collective-permute-done((bf16[16,24,128]{2,1,0:T(8,128)(2,1)S(1)}, bf16[16,24,128]{2,1,0:T(8,128)(2,1)S(1)}, u32[]{:S(2)}, u32[]{:S(2)}) %collective-permute-start.10) | collective-permute-done | bytes 98336 | tf_op jit(solution)/shard_map/ppermute | solution.py:45
  34.8 0.0 collective-permute-done.9.t_one
  34.8 0.9 %halo_3.1 = (f32[16,24,128]{2,1,0:T(8,128)S(1)}, f32[32,8,128]{2,1,0:T(8,128)S(1)}) custom-call(bf16[16,24,128]{2,1,0:T(8,128)(2,1)S(1)} %collective-permute-done.8.t_two, bf16[16,24,128]{2,1,0:T(8,128)(2,1)S(1)} %collective-permute-done.9.t_one, bf16[16,24,128]{2,1,0:T(8,128)(2,1)S(1)} %collective-permute-done.10.z_one, ...), custom_call_target="tpu_custom_call" | custom-call | tf_op jit(solution)/shard_map/halo_3/pallas_call | solution.py:556
  35.7 10.5 %all_to_all.5.sums = f32[32,8,128]{2,1,0:T(8,128)S(1)} all-to-all(f32[32,8,128]{2,1,0:T(8,128)S(1)} %get-tuple-element.39), channel_id=1, replica_groups=mesh['grp'=4,'dev'=8] {'grp','dev'}, dimensions={0} | all-to-all | bytes 262144 | tf_op jit(solution)/shard_map/all_to_all | solution.py:565
  46.2 3.2 %finish.1 = (bf16[16,24,2,3072]{3,2,1,0:T(2,128)(2,1)}, f32[16,24,128]{2,1,0:T(8,128)}) custom-call(f32[32,8,128]{2,1,0:T(8,128)S(1)} %all_to_all.5.sums, f32[16,24,128]{2,1,0:T(8,128)S(1)} %get-tuple-element.26.before.r0, f32[16,24,128]{2,1,0:T(8,128)S(1)} %get-tuple-element.32.before.v1, f32[16,24,128]{2,1,0:T(8,128)S(1)} %get-tuple-element.30.rest.w1, ...), custom_call_target="tpu_custom_call" | custom-call | tf_op jit(solution)/shard_map/finish/pallas_call | solution.py:473
  (9 shorter events, 0.0 us)
Async XLA Ops:
  5.6 9.1 %collective-permute-start.3 = (bf16[16,24,128]{2,1,0:T(8,128)(2,1)S(1)}, bf16[16,24,128]{2,1,0:T(8,128)(2,1)S(1)}, u32[]{:S(2)}, u32[]{:S(2)}) collective-permute-start(bf16[16,24,128]{2,1,0:T(8,128)(2,1)S(1)} %get-tuple-element.23.high), channel_id=1, source_target_pairs={{0,7},{1,2},{2,1},{3,4},{4,3},{5,6},{6,5},{7,0},{8,15},{9,10},{10,... | collective-permute-start | bytes 294920 | tf_op jit(solution)/shard_map/ppermute | solution.py:44
  11.7 4.9 %collective-permute-start.2 = (bf16[16,24,128]{2,1,0:T(8,128)(2,1)S(1)}, bf16[16,24,128]{2,1,0:T(8,128)(2,1)S(1)}, u32[]{:S(2)}, u32[]{:S(2)}) collective-permute-start(bf16[16,24,128]{2,1,0:T(8,128)(2,1)S(1)} %get-tuple-element.23.high), channel_id=1, source_target_pairs={{0,1},{1,0},{2,3},{3,2},{4,5},{5,4},{6,7},{7,6},{8,9},{9,8},{10,11... | collective-permute-start | bytes 294920 | tf_op jit(solution)/shard_map/ppermute | solution.py:45
  11.7 4.9 %collective-permute-start.1 = (bf16[16,24,128]{2,1,0:T(8,128)(2,1)S(1)}, bf16[16,24,128]{2,1,0:T(8,128)(2,1)S(1)}, u32[]{:S(2)}, u32[]{:S(2)}) collective-permute-start(bf16[16,24,128]{2,1,0:T(8,128)(2,1)S(1)} %get-tuple-element.23.high), channel_id=1, source_target_pairs={{0,24},{8,0},{16,8},{24,16},{1,25},{9,1},{17,9},{25,17},{2,26},{10... | collective-permute-start | bytes 294920 | tf_op jit(solution)/shard_map/ppermute | solution.py:46
  12.3 4.5 %collective-permute-start = (bf16[16,24,128]{2,1,0:T(8,128)(2,1)S(1)}, bf16[16,24,128]{2,1,0:T(8,128)(2,1)S(1)}, u32[]{:S(2)}, u32[]{:S(2)}) collective-permute-start(bf16[16,24,128]{2,1,0:T(8,128)(2,1)S(1)} %get-tuple-element.23.high), channel_id=1, source_target_pairs={{24,0},{0,8},{8,16},{16,24},{25,1},{1,9},{9,17},{17,25},{26,2},{2,... | collective-permute-start | bytes 294920 | tf_op jit(solution)/shard_map/ppermute | solution.py:43
  17.4 7.4 %collective-permute-start.7 = (bf16[16,24,128]{2,1,0:T(8,128)(2,1)S(1)}, bf16[16,24,128]{2,1,0:T(8,128)(2,1)S(1)}, u32[]{:S(2)}, u32[]{:S(2)}) collective-permute-start(bf16[16,24,128]{2,1,0:T(8,128)(2,1)S(1)} %get-tuple-element.28.high), channel_id=1, source_target_pairs={{0,7},{1,2},{2,1},{3,4},{4,3},{5,6},{6,5},{7,0},{8,15},{9,10},{10,... | collective-permute-start | bytes 294920 | tf_op jit(solution)/shard_map/ppermute | solution.py:44
  19.6 6.0 %collective-permute-start.6 = (bf16[16,24,128]{2,1,0:T(8,128)(2,1)S(1)}, bf16[16,24,128]{2,1,0:T(8,128)(2,1)S(1)}, u32[]{:S(2)}, u32[]{:S(2)}) collective-permute-start(bf16[16,24,128]{2,1,0:T(8,128)(2,1)S(1)} %get-tuple-element.28.high), channel_id=1, source_target_pairs={{0,1},{1,0},{2,3},{3,2},{4,5},{5,4},{6,7},{7,6},{8,9},{9,8},{10,11... | collective-permute-start | bytes 294920 | tf_op jit(solution)/shard_map/ppermute | solution.py:45
  19.6 6.0 %collective-permute-start.5 = (bf16[16,24,128]{2,1,0:T(8,128)(2,1)S(1)}, bf16[16,24,128]{2,1,0:T(8,128)(2,1)S(1)}, u32[]{:S(2)}, u32[]{:S(2)}) collective-permute-start(bf16[16,24,128]{2,1,0:T(8,128)(2,1)S(1)} %get-tuple-element.28.high), channel_id=1, source_target_pairs={{0,24},{8,0},{16,8},{24,16},{1,25},{9,1},{17,9},{25,17},{2,26},{10... | collective-permute-start | bytes 294920 | tf_op jit(solution)/shard_map/ppermute | solution.py:46
  19.6 6.0 %collective-permute-start.4 = (bf16[16,24,128]{2,1,0:T(8,128)(2,1)S(1)}, bf16[16,24,128]{2,1,0:T(8,128)(2,1)S(1)}, u32[]{:S(2)}, u32[]{:S(2)}) collective-permute-start(bf16[16,24,128]{2,1,0:T(8,128)(2,1)S(1)} %get-tuple-element.28.high), channel_id=1, source_target_pairs={{24,0},{0,8},{8,16},{16,24},{25,1},{1,9},{9,17},{17,25},{26,2},{2,... | collective-permute-start | bytes 294920 | tf_op jit(solution)/shard_map/ppermute | solution.py:43
  26.2 7.5 %collective-permute-start.11 = (bf16[16,24,128]{2,1,0:T(8,128)(2,1)S(1)}, bf16[16,24,128]{2,1,0:T(8,128)(2,1)S(1)}, u32[]{:S(2)}, u32[]{:S(2)}) collective-permute-start(bf16[16,24,128]{2,1,0:T(8,128)(2,1)S(1)} %get-tuple-element.33.high), channel_id=1, source_target_pairs={{0,7},{1,2},{2,1},{3,4},{4,3},{5,6},{6,5},{7,0},{8,15},{9,10},{10,... | collective-permute-start | bytes 294920 | tf_op jit(solution)/shard_map/ppermute | solution.py:44
  28.9 5.9 %collective-permute-start.10 = (bf16[16,24,128]{2,1,0:T(8,128)(2,1)S(1)}, bf16[16,24,128]{2,1,0:T(8,128)(2,1)S(1)}, u32[]{:S(2)}, u32[]{:S(2)}) collective-permute-start(bf16[16,24,128]{2,1,0:T(8,128)(2,1)S(1)} %get-tuple-element.33.high), channel_id=1, source_target_pairs={{0,1},{1,0},{2,3},{3,2},{4,5},{5,4},{6,7},{7,6},{8,9},{9,8},{10,11... | collective-permute-start | bytes 294920 | tf_op jit(solution)/shard_map/ppermute | solution.py:45
  28.9 5.9 %collective-permute-start.9 = (bf16[16,24,128]{2,1,0:T(8,128)(2,1)S(1)}, bf16[16,24,128]{2,1,0:T(8,128)(2,1)S(1)}, u32[]{:S(2)}, u32[]{:S(2)}) collective-permute-start(bf16[16,24,128]{2,1,0:T(8,128)(2,1)S(1)} %get-tuple-element.33.high), channel_id=1, source_target_pairs={{0,24},{8,0},{16,8},{24,16},{1,25},{9,1},{17,9},{25,17},{2,26},{10... | collective-permute-start | bytes 294920 | tf_op jit(solution)/shard_map/ppermute | solution.py:46
  28.9 5.9 %collective-permute-start.8 = (bf16[16,24,128]{2,1,0:T(8,128)(2,1)S(1)}, bf16[16,24,128]{2,1,0:T(8,128)(2,1)S(1)}, u32[]{:S(2)}, u32[]{:S(2)}) collective-permute-start(bf16[16,24,128]{2,1,0:T(8,128)(2,1)S(1)} %get-tuple-element.33.high), channel_id=1, source_target_pairs={{24,0},{0,8},{8,16},{16,24},{25,1},{1,9},{9,17},{17,25},{26,2},{2,... | collective-permute-start | bytes 294920 | tf_op jit(solution)/shard_map/ppermute | solution.py:43
